TPU v7x, 256 devices: a whole 4x4x8 slice. The times are simulated.
256 devices in a mesh: dp: 16 (over z, core), tensor: 16 (over x, y).
Axes of the slice: x: 4, y: 4, z: 8, core: 2. Of those that a mesh axis runs over, the one named last changes fastest.
Arguments:
- gate_grad: bfloat16 [16, 2048, 4096], P('dp', 'tensor'), may hold values from -6 to 6
- gate_scale: float32 [16, 2048, 32], P('dp', 'tensor'), may hold values from 0.4 to 8
- gate_error: bfloat16 [16, 2048, 4096], P('dp', 'tensor'), may hold values from -6 to 6
- gate_prior: float32 [4096, 32], replicated, may hold values from -6 to 6
- up_grad: bfloat16 [16, 2048, 4096], P('dp', 'tensor'), may hold values from -6 to 6
- up_scale: float32 [16, 2048, 32], P('dp', 'tensor'), may hold values from 0.4 to 8
- up_error: bfloat16 [16, 2048, 4096], P('dp', 'tensor'), may hold values from -6 to 6
- up_prior: float32 [4096, 32], replicated, may hold values from -6 to 6
Outputs:
- gate_columns: float32 [4096, 32], replicated
- up_columns: float32 [4096, 32], replicated
- gate_update: bfloat16 [2048, 4096], P('tensor')
- up_update: bfloat16 [2048, 4096], P('tensor')
- gate_residue: bfloat16 [16, 2048, 4096], P('dp', 'tensor')
- up_residue: bfloat16 [16, 2048, 4096], P('dp', 'tensor')
All inputs are finite; a program needn't handle non-finite values.
Results may differ from a plain program's by a relative error of at most 0.001.
Values sent between devices are 32-bit elements; how exact they have to be, the bound alone decides.
A program may use at most 64 MiB of HBM per device.

v0:
```python
import jax
import jax.numpy as jnp
from jax import lax
from jax.sharding import PartitionSpec as P


def expand(grad, scale):
    blocks = scale.shape[-1]
    width = grad.shape[-1] // blocks
    values = grad.astype(jnp.float32).reshape(grad.shape[:-1] + (blocks, width))
    return (values * scale[..., None]).reshape(grad.shape)


def settle(works, priors):
    partial_factor = jnp.einsum("krd,kdj->krj", works, priors, precision=lax.Precision.HIGHEST)
    factors = lax.psum(partial_factor, "dp")
    partial_gram = jnp.einsum("kri,krj->kij", factors, factors, precision=lax.Precision.HIGHEST)
    grams = lax.psum(partial_gram, "tensor")
    lower_factor = jnp.linalg.cholesky(grams)
    basis = lax.linalg.triangular_solve(
        lower_factor, factors, left_side=False, lower=True, transpose_a=True
    )
    terms = jnp.einsum("krd,krj->kdj", works, basis, precision=lax.Precision.HIGHEST)
    totals = lax.psum(terms, ("dp", "tensor"))
    columns = totals / float(lax.axis_size("dp"))
    approx = jnp.einsum("krj,kdj->krd", basis, columns, precision=lax.Precision.HIGHEST)
    return (columns, approx.astype(jnp.bfloat16), (works - approx).astype(jnp.bfloat16))


def shards(gate_grad, gate_scale, gate_error, gate_prior, up_grad, up_scale, up_error, up_prior):
    grads = jnp.concatenate((gate_grad, up_grad), 0)
    scales = jnp.concatenate((gate_scale, up_scale), 0)
    errors = jnp.concatenate((gate_error, up_error), 0)
    works = expand(grads, scales) + errors.astype(jnp.float32)
    priors = jnp.stack((gate_prior, up_prior))
    first = settle(works[0:1], priors[0:1])
    second = settle(works[1:2], priors[1:2])
    columns = jnp.concatenate((first[0], second[0]), 0)
    update = jnp.concatenate((first[1], second[1]), 0)
    residue = jnp.concatenate((first[2], second[2]), 0)
    return (columns[0], columns[1], update[0], update[1], residue[0:1], residue[1:2])


def solution(mesh):
    in_specs = (
        P("dp", "tensor", None),
        P("dp", "tensor", None),
        P("dp", "tensor", None),
        P(),
        P("dp", "tensor", None),
        P("dp", "tensor", None),
        P("dp", "tensor", None),
        P(),
    )
    out_specs = (
        P(),
        P(),
        P("tensor", None),
        P("tensor", None),
        P("dp", "tensor", None),
        P("dp", "tensor", None),
    )
    return jax.shard_map(shards, mesh=mesh, in_specs=in_specs, out_specs=out_specs, check_vma=False)
```

profile of v0, /device:TPU:1, one launch (start us, length us, event | category | flops | bytes accessed | tf_op | source)
XLA Modules:
  0.0 436.0 jit_solution(8131022795377205813)
XLA Ops:
  7.2 0.0 copy-start
  7.2 0.0 all-reduce.5.cloned.1.call-start
  7.2 0.8 pad_maximum_fusion
  8.0 0.1 copy.14
  8.1 2.6 mul.11
  10.7 0.0 copy-start.5
  10.7 5.1 %mul.12 = f32[2,128,4096]{2,1,0:T(8,128)} reshape(f32[2,128,32,128]{3,2,1,0:T(8,128)} %mul.11) | data formatting | bytes 8388608 | tf_op jit(solution)/shard_map/mul | solution.py:11
  15.8 0.0 copy-done.5
  15.8 0.0 copy-done.6
  15.8 3.6 convert_add_fusion
  19.4 0.0 copy-done
  19.4 0.0 copy-start.1
  19.4 0.0 copy-start.7
  19.4 2.1 fusion.12
  21.5 0.0 copy-done.1
  21.5 0.0 copy-done.7
  21.5 2.1 fusion.15
  23.6 48.8 %all-reduce.2 = (f32[1,128,32]{1,2,0:T(8,128)S(1)}, f32[1,128,32]{1,2,0:T(8,128)S(1)}) all-reduce(f32[1,128,32]{1,2,0:T(8,128)S(1)} %fusion.12, f32[1,128,32]{1,2,0:T(8,128)S(1)} %fusion.15), channel_id=1, replica_groups=mesh['dp'=16,'tensor'=16] {'dp'}, use_global_device_ids=true, to_apply=%region_0.0 | all-reduce | flops 8192 | bytes 65536 | tf_op jit(solution)/shard_map/psum | solution.py:16
  72.4 0.1 convolution_bitcast_fusion.5
  72.6 0.1 convolution_bitcast_fusion.3
  72.7 60.7 %all-reduce.1 = (f32[1,32,32]{1,2,0:T(8,128)S(1)}, f32[1,32,32]{1,2,0:T(8,128)S(1)}) all-reduce(f32[1,32,32]{1,2,0:T(8,128)S(1)} %convolution_bitcast_fusion.5, f32[1,32,32]{1,2,0:T(8,128)S(1)} %convolution_bitcast_fusion.3), channel_id=1, replica_groups=mesh['dp'=16,'tensor'=16] {'tensor'}, use_global_device_ids=true, to_apply=%region_1.0 | all-reduce | flops 2048 | bytes 16384 | tf_op jit(solution)/shard_map/psum | solution.py:18
  133.5 0.1 copy.18
  133.5 0.1 copy.16
  133.6 2.9 custom-call.8
  136.6 0.6 compare_reduce_fusion.1
  137.2 0.7 fusion.18
  137.9 2.4 custom-call.9
  140.3 0.2 convolution_bitcast_fusion.4
  140.6 3.6 convolution_bitcast_fusion.1
  144.2 2.9 custom-call.10
  147.1 0.6 compare_reduce_fusion
  147.8 0.7 fusion.19
  148.4 2.4 custom-call.11
  150.9 0.2 convolution_bitcast_fusion.2
  151.1 3.6 convolution_bitcast_fusion
  154.7 0.0 all-reduce.5.cloned.1.call-update
  154.8 264.6 %all-reduce.5.cloned.1.call-done = (f32[1,4096,32]{1,2,0:T(8,128)}, f32[1,4096,32]{1,2,0:T(8,128)}) async-done(((f32[1,4096,32]{1,2,0:T(8,128)}, f32[1,4096,32]{1,2,0:T(8,128)}), (f32[1,4096,32]{1,2,0:T(8,128)}, f32[1,4096,32]{1,2,0:T(8,128)})) %all-reduce.5.cloned.1.call-update) | async-done | bytes 1048592 | tf_op jit(solution)/shard_map/psum | solution.py:24
  419.3 1.1 multiply_bitcast_fusion.1
  420.4 0.0 copy-start.3
  420.4 1.3 multiply_bitcast_fusion
  421.7 0.0 copy-start.4
  421.7 0.0 copy-start.2
  421.7 2.8 fusion.28
  424.5 0.0 copy-done.3
  424.5 2.8 fusion.29
  427.3 0.0 copy-done.4
  427.3 0.0 copy-done.2
  427.3 1.8 fusion
  (4 shorter events, 0.1 us)
Async XLA Ops:
  7.2 12.2 %copy-start = (f32[4096,32]{0,1:T(8,128)S(1)}, f32[4096,32]{0,1:T(8,128)}, u32[]{:S(2)}) copy-start(f32[4096,32]{0,1:T(8,128)} %param.14) | copy-start | bytes 1572868
  7.2 412.1 %all-reduce.5.cloned.1.call-start = ((), (), s32[]{:S(2)}) async-start(), calls=%async_computation | async-start | bytes 2097152 | tf_op jit(solution)/shard_map/psum | solution.py:24
  10.7 5.1 %copy-start.5 = (bf16[1,128,4096]{2,1,0:T(8,128)(2,1)S(1)}, bf16[1,128,4096]{2,1,0:T(8,128)(2,1)}, u32[]{:S(2)}) copy-start(bf16[1,128,4096]{2,1,0:T(8,128)(2,1)} %param.15) | copy-start | bytes 3145732
  10.7 5.1 %copy-start.6 = (bf16[1,128,4096]{2,1,0:T(8,128)(2,1)S(1)}, bf16[1,128,4096]{2,1,0:T(8,128)(2,1)}, u32[]{:S(2)}) copy-start(bf16[1,128,4096]{2,1,0:T(8,128)(2,1)} %param.11) | copy-start | bytes 3145732
  19.4 2.1 copy-start.1
  19.4 2.1 copy-start.7
  420.4 4.1 copy-start.3
  421.7 5.6 %copy-start.4 = (f32[4096,32]{0,1:T(8,128)}, f32[4096,32]{0,1:T(8,128)S(1)}, u32[]{:S(2)}) copy-start(f32[4096,32]{0,1:T(8,128)S(1)} %multiply_bitcast_fusion) | copy-start | bytes 1572868
  421.7 5.6 %copy-start.2 = (f32[2,128,4096]{2,1,0:T(8,128)S(1)}, f32[2,128,4096]{2,1,0:T(8,128)}, u32[]{:S(2)}) copy-start(f32[2,128,4096]{2,1,0:T(8,128)} %copy-done.1) | copy-start | bytes 12582916
Sparse Core Ops, SparseCore 0:
  154.9 264.3 all-reduce.4
where the time goes:
time: 437 us; the launch traced here: 436 us
  waiting for transfers between devices  265 us (61%)
  blocking collectives  110 us (25%)
  other arithmetic  21.9 us (5%)
  matrix products  17.8 us (4%)
  between operations  14.2 us (3%)
  local copies, waits for them, and re-layouts  7.96 us (2%)
    psum x1, waiting for transfers between devices, settle(): totals = lax.psum(terms, ('dp', 'tensor'))  265 us
    psum x1, blocking collectives, settle(): grams = lax.psum(partial_gram, 'tensor')  60.7 us
    psum x1, blocking collectives, settle(): factors = lax.psum(partial_factor, 'dp')  48.8 us
  transfers between devices with their start and end apart: 1, of which 1 were waited for; matrix products, arithmetic and copies ran while one was open for 0% of the time, Pallas kernels for 0%

commit v1 on v0

v1 whole, which is shorter than its diff:
```python
import functools

import jax
import jax.numpy as jnp
from jax import lax
from jax.experimental import pallas as pl
from jax.experimental.pallas import tpu as pltpu
from jax.sharding import PartitionSpec as P

MESH = pl.DeviceIdType.MESH
F32 = jnp.float32
BF16 = jnp.bfloat16

ROWS = 128
COLS = 4096
RANK = 32
BLOCK = 128
NZ = 8
NXY = 16
HALVES = 2
SPAN = COLS // HALVES
PIECE = SPAN // NXY
CHUNKS = 4
WIDTH = COLS // CHUNKS

NN = (((1,), (0,)), ((), ()))
NT = (((1,), (1,)), ((), ()))


def split2(a):
    hi = a.astype(BF16)
    lo = (a - hi.astype(F32)).astype(BF16)
    return hi, lo


def split3(a):
    hi = a.astype(BF16)
    rest = a - hi.astype(F32)
    mid = rest.astype(BF16)
    lo = (rest - mid.astype(F32)).astype(BF16)
    return hi, mid, lo


def mm(a, b, dims=NN):
    return lax.dot_general(a, b, dims, preferred_element_type=F32)


def exact(a, b, dims=NN):
    return lax.dot_general(a, b, dims, preferred_element_type=F32, precision=lax.Precision.HIGHEST)


def inverse_factor(gram):
    rows = lax.broadcasted_iota(jnp.int32, (RANK, 1), 0)
    eye = (lax.broadcasted_iota(jnp.int32, (RANK, RANK), 0) == lax.broadcasted_iota(jnp.int32, (RANK, RANK), 1)).astype(F32)
    left, right = gram, eye
    roots = jnp.zeros((RANK, 1), F32)
    for j in range(RANK):
        pivot = left[j : j + 1, j : j + 1]
        roots = jnp.where(rows == j, lax.rsqrt(pivot), roots)
        factor = jnp.where(rows > j, left[:, j : j + 1] / pivot, 0.0)
        left = left - factor * left[j : j + 1, :]
        right = right - factor * right[j : j + 1, :]
    return right * roots


def total_wait(ref, sem):
    pltpu.make_async_copy(ref, ref, sem).wait()


def exchange_kernel(
    g0, s0, e0, p0, g1, s1, e1, p1,
    columns0, columns1, basis,
    g_buf, e_buf, s_buf, p_buf, w_hi, w_lo,
    f_part, f_pair, f_own, f_z, f_all, gram_own, gram_xy,
    t_own, t_pair, t_xy, t_z, piece,
    in_sems, pair_send, pair_recv, z_send, z_recv, xy_send, xy_recv, t_send, t_recv,
):
    dp = lax.axis_index("dp")
    me = lax.axis_index("tensor")
    z, c = dp // 2, dp % 2
    x, y = me // 4, me % 4
    other = 1 - c
    sibling = {"dp": z * 2 + other, "tensor": me}
    z_peers = [{"dp": lax.rem(z + k, NZ) * 2 + c, "tensor": me} for k in (4, 3, 5, 2, 6, 1, 7)]
    xy_index = [
        lax.rem(x + dx, 4) * 4 + lax.rem(y + dy, 4)
        for dx, dy in sorted(
            ((i, j) for i in range(4) for j in range(4) if i or j),
            key=lambda d: -(min(d[0], 4 - d[0]) + min(d[1], 4 - d[1])),
        )
    ]
    xy_peers = [{"dp": dp, "tensor": t} for t in xy_index]

    barrier = pltpu.get_barrier_semaphore()
    for peer in [sibling] + z_peers + xy_peers:
        pl.semaphore_signal(barrier, inc=1, device_id=peer, device_id_type=MESH)

    small = []
    for m, (s, p) in enumerate(((s0, p0), (s1, p1))):
        small.append(pltpu.make_async_copy(s.at[0], s_buf.at[m], in_sems.at[m, 0]))
        small.append(pltpu.make_async_copy(p, p_buf.at[m], in_sems.at[m, 1]))
    for copy in small:
        copy.start()
    big = {}
    for m, (g, e) in enumerate(((g0, e0), (g1, e1))):
        for k in range(CHUNKS):
            cols = pl.ds(k * WIDTH, WIDTH)
            big[m, k] = (
                pltpu.make_async_copy(g.at[0, :, cols], g_buf.at[m, :, cols], in_sems.at[m, 2 + 2 * k]),
                pltpu.make_async_copy(e.at[0, :, cols], e_buf.at[m, :, cols], in_sems.at[m, 3 + 2 * k]),
            )
            for copy in big[m, k]:
                copy.start()
    for copy in small:
        copy.wait()

    for m in range(2):
        scale = s_buf[m].T
        total = jnp.zeros((ROWS, 3 * RANK), F32)
        for k in range(CHUNKS):
            for copy in big[m, k]:
                copy.wait()
            for b in range(k * WIDTH // BLOCK, (k + 1) * WIDTH // BLOCK):
                cols = slice(b * BLOCK, (b + 1) * BLOCK)
                work = g_buf[m, :, cols].astype(F32) * scale[:, b : b + 1] + e_buf[m, :, cols].astype(F32)
                hi, lo = split2(work)
                w_hi[m, :, cols] = hi
                w_lo[m, :, cols] = lo
            cols = slice(k * WIDTH, (k + 1) * WIDTH)
            prior = jnp.concatenate(split3(p_buf[m, :, cols]), 0)
            total = total + mm(w_hi[m, :, cols], prior, NT) + mm(w_lo[m, :, cols], prior, NT)
        factor = total[:, :RANK] + (total[:, RANK : 2 * RANK] + total[:, 2 * RANK :])
        f_part[m] = factor.T

    pl.semaphore_wait(barrier, 1 + len(z_peers) + len(xy_peers))

    sends = []

    def send(src, dst, send_sem, recv_sem, peer):
        copy = pltpu.make_async_remote_copy(
            src_ref=src, dst_ref=dst, send_sem=send_sem, recv_sem=recv_sem, device_id=peer, device_id_type=MESH
        )
        copy.start()
        return copy

    first = send(f_part.at[other], f_pair, pair_send.at[0], pair_recv.at[0], sibling)
    sends.append(first)
    first.wait_recv()
    f_own[...] = f_part[c] + f_pair[...]
    f_z[z] = f_own[...]

    for peer in z_peers:
        send(f_own, f_z.at[z], z_send.at[0], z_recv.at[0], peer)
    total_wait(f_z.at[pl.ds(0, NZ - 1)], z_recv.at[0])
    mine = f_z[0]
    for k in range(1, NZ):
        mine = mine + f_z[k]
    f_all[c] = mine
    second = send(f_all.at[c], f_all.at[c], pair_send.at[1], pair_recv.at[1], sibling)
    sends.append(second)

    gram = exact(mine, mine, NT)
    gram_own[...] = jnp.concatenate([gram, jnp.zeros((RANK, 128 - RANK), F32)], 1)
    gram_xy[me] = gram_own[...]
    for peer in xy_peers:
        send(gram_own, gram_xy.at[me], xy_send.at[0], xy_recv.at[0], peer)

    def terms(m, factor, span):
        hi, lo = split2(factor)
        zero = jnp.zeros_like(lo)
        lhs = jnp.concatenate([jnp.concatenate([hi, hi], 1), jnp.concatenate([lo, zero], 1)], 0)
        rhs = jnp.concatenate([w_hi[m, :, span], w_lo[m, :, span]], 0)
        both = mm(lhs, rhs)
        return both[:RANK] + both[RANK:]

    for h in range(HALVES):
        t_own[h] = terms(c, mine, pl.ds(h * SPAN, SPAN))
    second.wait_recv()
    theirs = f_all[other]
    pair_copies = []
    for h in range(HALVES):
        t_pair[0, h] = terms(other, theirs, pl.ds(h * SPAN, SPAN))
        pair_copies.append(send(t_pair.at[0, h], t_pair.at[1, h], pair_send.at[2 + h], pair_recv.at[2 + h], sibling))
    sends += pair_copies

    for h in range(HALVES):
        pair_copies[h].wait_recv()
        t_own[h] = t_own[h] + t_pair[1, h]
        for t, peer in zip(xy_index, xy_peers):
            cols = pl.ds(pl.multiple_of(t * PIECE, PIECE), PIECE)
            send(t_own.at[h, :, cols], t_xy.at[h, me], t_send.at[0, h], t_recv.at[0, h], peer)
        t_xy[h, me] = t_own[h, :, pl.ds(pl.multiple_of(me * PIECE, PIECE), PIECE)]

    total_wait(gram_xy.at[pl.ds(0, NXY - 1)], xy_recv.at[0])
    gram = gram_xy[0]
    for k in range(1, NXY):
        gram = gram + gram_xy[k]
    inverse = inverse_factor(gram[:, :RANK])
    basis[c] = exact(inverse, mine)
    sends.append(send(basis.at[c], basis.at[c], pair_send.at[4], pair_recv.at[4], sibling))

    for h in range(HALVES):
        total_wait(t_xy.at[h, pl.ds(0, NXY - 1)], t_recv.at[0, h])
        part = t_xy[h, 0]
        for k in range(1, NXY):
            part = part + t_xy[h, k]
        piece[0, h] = part
        t_z[h, z] = part
        for peer in z_peers:
            send(piece.at[0, h], t_z.at[h, z], t_send.at[1, h], t_recv.at[1, h], peer)

    for h in range(HALVES):
        total_wait(t_z.at[h, pl.ds(0, NZ - 1)], t_recv.at[1, h])
        part = t_z[h, 0]
        for k in range(1, NZ):
            part = part + t_z[h, k]
        piece[1, h] = exact(inverse, part) * (1.0 / 16.0)
        cols = pl.ds(pl.multiple_of(h * SPAN + me * PIECE, PIECE), PIECE)

        @pl.when(c == 0)
        def _():
            columns0[:, cols] = piece[1, h]
            for peer in xy_peers:
                send(piece.at[1, h], columns0.at[:, cols], t_send.at[2, h], t_recv.at[2, h], peer)

        @pl.when(c == 1)
        def _():
            columns1[:, cols] = piece[1, h]
            for peer in xy_peers:
                send(piece.at[1, h], columns1.at[:, cols], t_send.at[2, h], t_recv.at[2, h], peer)

    for h in range(HALVES):
        total_wait(t_xy.at[h, pl.ds(0, NXY - 1)], t_recv.at[2, h])
        cols = pl.ds(h * SPAN, SPAN)

        @pl.when(c == 0)
        def _():
            send(columns0.at[:, cols], columns0.at[:, cols], pair_send.at[5 + h], pair_recv.at[5 + h], sibling)

        @pl.when(c == 1)
        def _():
            send(columns1.at[:, cols], columns1.at[:, cols], pair_send.at[5 + h], pair_recv.at[5 + h], sibling)

    for h in range(HALVES):
        total_wait(t_own.at[h], pair_recv.at[5 + h])
        total_wait(t_own.at[h], pair_send.at[5 + h])
    sends[-1].wait_recv()
    for copy in sends:
        copy.wait_send()
    total_wait(f_z.at[pl.ds(0, NZ - 1)], z_send.at[0])
    total_wait(gram_xy.at[pl.ds(0, NXY - 1)], xy_send.at[0])
    for h in range(HALVES):
        total_wait(t_xy.at[h, pl.ds(0, NXY - 1)], t_send.at[0, h])
        total_wait(t_z.at[h, pl.ds(0, NZ - 1)], t_send.at[1, h])
        total_wait(t_xy.at[h, pl.ds(0, NXY - 1)], t_send.at[2, h])


def exchange(*args):
    vmem, sems = pltpu.VMEM, pltpu.SemaphoreType.DMA
    return pl.pallas_call(
        exchange_kernel,
        out_shape=(
            jax.ShapeDtypeStruct((RANK, COLS), F32),
            jax.ShapeDtypeStruct((RANK, COLS), F32),
            jax.ShapeDtypeStruct((2, RANK, ROWS), F32),
        ),
        in_specs=[pl.BlockSpec(memory_space=pl.ANY)] * 8,
        out_specs=[pl.BlockSpec(memory_space=pltpu.VMEM)] * 3,
        scratch_shapes=[
            vmem((2, ROWS, COLS), BF16),
            vmem((2, ROWS, COLS), BF16),
            vmem((2, COLS // BLOCK, ROWS), F32),
            vmem((2, RANK, COLS), F32),
            vmem((2, ROWS, COLS), BF16),
            vmem((2, ROWS, COLS), BF16),
            vmem((2, RANK, ROWS), F32),
            vmem((RANK, ROWS), F32),
            vmem((RANK, ROWS), F32),
            vmem((NZ, RANK, ROWS), F32),
            vmem((2, RANK, ROWS), F32),
            vmem((RANK, 128), F32),
            vmem((NXY, RANK, 128), F32),
            vmem((HALVES, RANK, SPAN), F32),
            vmem((2, HALVES, RANK, SPAN), F32),
            vmem((HALVES, NXY, RANK, PIECE), F32),
            vmem((HALVES, NZ, RANK, PIECE), F32),
            vmem((2, HALVES, RANK, PIECE), F32),
            sems((2, 2 + 2 * CHUNKS)),
            sems((5 + HALVES,)),
            sems((5 + HALVES,)),
            sems((1,)),
            sems((1,)),
            sems((1,)),
            sems((1,)),
            sems((3, HALVES)),
            sems((3, HALVES)),
        ],
        compiler_params=pltpu.CompilerParams(collective_id=0, has_side_effects=True, vmem_limit_bytes=28 << 20),
        cost_estimate=pl.CostEstimate(flops=1 << 30, bytes_accessed=8 << 20, transcendentals=0),
    )(*args)


def finish_kernel(
    g0, s0, e0, g1, s1, e1, columns0, columns1, basis,
    out0, out1, update0, update1, residue0, residue1,
):
    step = pl.program_id(0)
    for m, (g, s, e, columns, out, update, residue) in enumerate(
        ((g0, s0, e0, columns0, out0, update0, residue0), (g1, s1, e1, columns1, out1, update1, residue1))
    ):
        block = columns[...]
        out[...] = block
        approx = exact(basis[m].T, block)
        update[...] = approx.astype(BF16)
        width = block.shape[1]
        count = width // BLOCK
        scale = s[0, pl.ds(pl.multiple_of(step * count, count), count), :].T
        for b in range(count):
            cols = slice(b * BLOCK, (b + 1) * BLOCK)
            work = g[0, :, cols].astype(F32) * scale[:, b : b + 1] + e[0, :, cols].astype(F32)
            residue[0, :, cols] = (work - approx[:, cols]).astype(BF16)


def finish(g0, s0, e0, g1, s1, e1, columns0, columns1, basis):
    width = 1024
    grad = pl.BlockSpec((1, ROWS, width), lambda i: (0, 0, i))
    scale = pl.BlockSpec((1, COLS // BLOCK, ROWS), lambda i: (0, 0, 0))
    column = pl.BlockSpec((RANK, width), lambda i: (0, i))
    wide = pl.BlockSpec((ROWS, width), lambda i: (0, i))
    return pl.pallas_call(
        finish_kernel,
        grid=(COLS // width,),
        out_shape=(
            jax.ShapeDtypeStruct((RANK, COLS), F32),
            jax.ShapeDtypeStruct((RANK, COLS), F32),
            jax.ShapeDtypeStruct((ROWS, COLS), BF16),
            jax.ShapeDtypeStruct((ROWS, COLS), BF16),
            jax.ShapeDtypeStruct((1, ROWS, COLS), BF16),
            jax.ShapeDtypeStruct((1, ROWS, COLS), BF16),
        ),
        in_specs=[grad, scale, grad, grad, scale, grad, column, column, pl.BlockSpec((2, RANK, ROWS), lambda i: (0, 0, 0))],
        out_specs=[column, column, wide, wide, grad, grad],
        compiler_params=pltpu.CompilerParams(vmem_limit_bytes=28 << 20),
    )(g0, s0, e0, g1, s1, e1, columns0, columns1, basis)


def shards(gate_grad, gate_scale, gate_error, gate_prior, up_grad, up_scale, up_error, up_prior):
    s0, s1 = (s.transpose(0, 2, 1) for s in (gate_scale, up_scale))
    columns0, columns1, basis = exchange(
        gate_grad, s0, gate_error, gate_prior.T, up_grad, s1, up_error, up_prior.T
    )
    columns0, columns1, update0, update1, residue0, residue1 = finish(
        gate_grad, s0, gate_error, up_grad, s1, up_error, columns0, columns1, basis
    )
    return (columns0.T, columns1.T, update0, update1, residue0, residue1)


def solution(mesh):
    in_specs = (
        P("dp", "tensor", None),
        P("dp", "tensor", None),
        P("dp", "tensor", None),
        P(),
        P("dp", "tensor", None),
        P("dp", "tensor", None),
        P("dp", "tensor", None),
        P(),
    )
    out_specs = (
        P(),
        P(),
        P("tensor", None),
        P("tensor", None),
        P("dp", "tensor", None),
        P("dp", "tensor", None),
    )
    return jax.shard_map(shards, mesh=mesh, in_specs=in_specs, out_specs=out_specs, check_vma=False)
```

time: 437 us -> 59.1 us (0.14)
  waiting for transfers between devices: 265 us -> 0 us
  blocking collectives: 110 us -> 0 us
  Pallas kernels: 0 us -> 49.6 us
  other arithmetic: 21.9 us -> 0 us
  matrix products: 17.8 us -> 0 us
  between operations: 14.2 us -> 0.68 us
    psum x1 -> x0, waiting for transfers between devices: 265 us -> none  [settle(): totals = lax.psum(terms, ('dp', 'tensor'))]
    psum x2 -> x0, blocking collectives: 110 us -> none  [the longest x1 60.7 us: settle(): grams = lax.psum(partial_gram, 'tensor')]
    pallas_call x0 -> x2, Pallas kernels: none -> 49.6 us  [the longest x1 43.7 us: exchange(): pl.pallas_call(exchange_kernel, out_shape=(jax.ShapeDtypeStruct((RANK, CO...]
    dot_general x8 -> x0, matrix products: 17.3 us -> none  [the longest x2 7.26 us: settle(): jnp.einsum('krd,krj->kdj', works, basis, precision=lax.Precision.HIGHEST)]
    another operation x10 -> x0, other arithmetic: 13.3 us -> none  [the longest x6 7.18 us: settle(): lower_factor = jnp.linalg.cholesky(grams)]
    unnamed x16 -> x20, local copies, waits for them, and re-layouts: 0.04 us -> 8.41 us
    mul x2 -> x0, local copies, waits for them, and re-layouts: 7.67 us -> none  [expand(): return (values * scale[..., None]).reshape(grad.shape)]
  transfers between devices with their start and end apart: 1 -> 0, of which waited for: 1 -> 0; matrix products, arithmetic and copies ran while one was open for 0% -> 0% of each run, Pallas kernels for 0% -> 0%
where the time goes in v1:
time: 59.1 us; the launch traced here: 58.7 us
  Pallas kernels  49.6 us (84%)
  local copies, waits for them, and re-layouts  8.41 us (14%)
  between operations  0.68 us (1%)
    pallas_call x1, Pallas kernels, exchange(): pl.pallas_call(exchange_kernel, out_shape=(jax.ShapeDtypeStruct((RANK, CO...  43.7 us
    unnamed x20, local copies, waits for them, and re-layouts  8.41 us
    pallas_call x1, Pallas kernels, finish(): pl.pallas_call(finish_kernel, grid=(COLS // width,), out_shape=(jax.Shape...  5.89 us

profile of v1, /device:TPU:1, one launch (start us, length us, event | category | flops | bytes accessed | tf_op | source)
XLA Modules:
  0.0 58.7 jit_solution(11697890542597632083)
XLA Ops:
  0.6 0.0 copy-start
  0.6 1.2 %copy-done = bf16[1,128,4096]{2,1,0:T(8,128)(2,1)S(1)} copy-done((bf16[1,128,4096]{2,1,0:T(8,128)(2,1)S(1)}, bf16[1,128,4096]{2,1,0:T(8,128)(2,1)}, u32[]{:S(2)}) %copy-start) | copy-done | bytes 1048600
  1.9 0.0 copy-start.1
  1.9 1.2 %copy-done.1 = bf16[1,128,4096]{2,1,0:T(8,128)(2,1)S(1)} copy-done((bf16[1,128,4096]{2,1,0:T(8,128)(2,1)S(1)}, bf16[1,128,4096]{2,1,0:T(8,128)(2,1)}, u32[]{:S(2)}) %copy-start.1) | copy-done | bytes 1048600
  3.1 0.0 copy-start.2
  3.1 1.2 %copy-done.2 = bf16[1,128,4096]{2,1,0:T(8,128)(2,1)S(1)} copy-done((bf16[1,128,4096]{2,1,0:T(8,128)(2,1)S(1)}, bf16[1,128,4096]{2,1,0:T(8,128)(2,1)}, u32[]{:S(2)}) %copy-start.2) | copy-done | bytes 1048600
  4.3 0.0 copy-start.4
  4.3 1.2 %copy-done.4 = bf16[1,128,4096]{2,1,0:T(8,128)(2,1)S(1)} copy-done((bf16[1,128,4096]{2,1,0:T(8,128)(2,1)S(1)}, bf16[1,128,4096]{2,1,0:T(8,128)(2,1)}, u32[]{:S(2)}) %copy-start.4) | copy-done | bytes 1048600
  5.5 0.0 copy-start.6
  5.5 1.0 %copy-done.6 = f32[4096,32]{0,1:T(8,128)S(1)} copy-done((f32[4096,32]{0,1:T(8,128)S(1)}, f32[4096,32]{0,1:T(8,128)}, u32[]{:S(2)}) %copy-start.6) | copy-done | bytes 524312
  6.6 0.0 copy-start.7
  6.6 1.0 %copy-done.7 = f32[4096,32]{0,1:T(8,128)S(1)} copy-done((f32[4096,32]{0,1:T(8,128)S(1)}, f32[4096,32]{0,1:T(8,128)}, u32[]{:S(2)}) %copy-start.7) | copy-done | bytes 524312
  7.6 0.0 copy-start.8
  7.6 0.7 %copy-done.8 = f32[1,128,32]{1,2,0:T(8,128)S(1)} copy-done((f32[1,128,32]{1,2,0:T(8,128)S(1)}, f32[1,128,32]{1,2,0:T(8,128)}, u32[]{:S(2)}) %copy-start.8) | copy-done | bytes 16408
  8.3 0.0 copy-start.9
  8.3 0.7 %copy-done.9 = f32[1,128,32]{1,2,0:T(8,128)S(1)} copy-done((f32[1,128,32]{1,2,0:T(8,128)S(1)}, f32[1,128,32]{1,2,0:T(8,128)}, u32[]{:S(2)}) %copy-start.9) | copy-done | bytes 16408
  9.1 0.0 copy-start.3
  9.1 0.0 copy-start.5
  9.1 43.7 %shard_map.127 = (f32[32,4096]{1,0:T(8,128)S(1)}, f32[32,4096]{1,0:T(8,128)S(1)}, f32[2,32,128]{2,1,0:T(8,128)S(1)}) custom-call(bf16[1,128,4096]{2,1,0:T(8,128)(2,1)S(1)} %copy-done, f32[1,32,128]{2,1,0:T(8,128)S(1)} %bitcast.8, bf16[1,128,4096]{2,1,0:T(8,128)(2,1)S(1)} %copy-done.1, f32[32,4096]{1,0:T(8,128)S(1)} %bitcast.6, ...), custom_call_target="tpu_custom_call" | custom-call | flops 1073741824 | bytes 8388608 | tf_op jit(solution)/shard_map/pallas_call | solution.py:260
  52.8 0.0 copy-done.3
  52.8 0.0 copy-done.5
  52.8 5.9 %shard_map.128 = (f32[32,4096]{1,0:T(8,128)}, f32[32,4096]{1,0:T(8,128)}, bf16[128,4096]{1,0:T(8,128)(2,1)}, bf16[128,4096]{1,0:T(8,128)(2,1)}, bf16[1,128,4096]...) custom-call(bf16[1,128,4096]{2,1,0:T(8,128)(2,1)S(1)} %copy-done, f32[1,32,128]{2,1,0:T(8,128)S(1)} %bitcast.9, ...), custom_call_target="tpu_custom_call" | custom-call | tf_op jit(solution)/shard_map/pallas_call | solution.py:330
Async XLA Ops:
  0.6 1.2 %copy-start = (bf16[1,128,4096]{2,1,0:T(8,128)(2,1)S(1)}, bf16[1,128,4096]{2,1,0:T(8,128)(2,1)}, u32[]{:S(2)}) copy-start(bf16[1,128,4096]{2,1,0:T(8,128)(2,1)} %g0.3) | copy-start | bytes 3145732
  1.9 1.2 %copy-start.1 = (bf16[1,128,4096]{2,1,0:T(8,128)(2,1)S(1)}, bf16[1,128,4096]{2,1,0:T(8,128)(2,1)}, u32[]{:S(2)}) copy-start(bf16[1,128,4096]{2,1,0:T(8,128)(2,1)} %e0.3) | copy-start | bytes 3145732
  3.1 1.2 %copy-start.2 = (bf16[1,128,4096]{2,1,0:T(8,128)(2,1)S(1)}, bf16[1,128,4096]{2,1,0:T(8,128)(2,1)}, u32[]{:S(2)}) copy-start(bf16[1,128,4096]{2,1,0:T(8,128)(2,1)} %g1.3) | copy-start | bytes 3145732
  4.3 1.2 %copy-start.4 = (bf16[1,128,4096]{2,1,0:T(8,128)(2,1)S(1)}, bf16[1,128,4096]{2,1,0:T(8,128)(2,1)}, u32[]{:S(2)}) copy-start(bf16[1,128,4096]{2,1,0:T(8,128)(2,1)} %e1.3) | copy-start | bytes 3145732
  5.5 1.0 %copy-start.6 = (f32[4096,32]{0,1:T(8,128)S(1)}, f32[4096,32]{0,1:T(8,128)}, u32[]{:S(2)}) copy-start(f32[4096,32]{0,1:T(8,128)} %param.11) | copy-start | bytes 1572868
  6.6 1.0 %copy-start.7 = (f32[4096,32]{0,1:T(8,128)S(1)}, f32[4096,32]{0,1:T(8,128)}, u32[]{:S(2)}) copy-start(f32[4096,32]{0,1:T(8,128)} %param.15) | copy-start | bytes 1572868
  7.6 0.7 %copy-start.8 = (f32[1,128,32]{1,2,0:T(8,128)S(1)}, f32[1,128,32]{1,2,0:T(8,128)}, u32[]{:S(2)}) copy-start(f32[1,128,32]{1,2,0:T(8,128)} %param.9) | copy-start | bytes 49156
  8.3 0.7 %copy-start.9 = (f32[1,128,32]{1,2,0:T(8,128)S(1)}, f32[1,128,32]{1,2,0:T(8,128)}, u32[]{:S(2)}) copy-start(f32[1,128,32]{1,2,0:T(8,128)} %param.13) | copy-start | bytes 49156
  9.1 43.7 %copy-start.3 = (bf16[1,128,4096]{2,1,0:T(8,128)(2,1)S(1)}, bf16[1,128,4096]{2,1,0:T(8,128)(2,1)}, u32[]{:S(2)}) copy-start(bf16[1,128,4096]{2,1,0:T(8,128)(2,1)} %g1.3) | copy-start | bytes 3145732
  9.1 43.7 %copy-start.5 = (bf16[1,128,4096]{2,1,0:T(8,128)(2,1)S(1)}, bf16[1,128,4096]{2,1,0:T(8,128)(2,1)}, u32[]{:S(2)}) copy-start(bf16[1,128,4096]{2,1,0:T(8,128)(2,1)} %e1.3) | copy-start | bytes 3145732

commit v2 on v0

v2 whole, which is shorter than its diff:
```python
import jax
import jax.numpy as jnp
from jax import lax
from jax.experimental import pallas as pl
from jax.experimental.pallas import tpu as pltpu
from jax.sharding import PartitionSpec as P

MESH = pl.DeviceIdType.MESH
F32 = jnp.float32
BF16 = jnp.bfloat16

ROWS = 128
COLS = 4096
RANK = 32
BLOCK = 128
NZ = 8
NXY = 16
PARTS = 4
RANKS = RANK // PARTS
PIECE = COLS // NXY
CHUNKS = 4
WIDTH = COLS // CHUNKS
SLICES = 8
SLICE = COLS // SLICES

NN = (((1,), (0,)), ((), ()))
NT = (((1,), (1,)), ((), ()))


def split2(a):
    hi = a.astype(BF16)
    lo = (a - hi.astype(F32)).astype(BF16)
    return hi, lo


def split3(a):
    hi = a.astype(BF16)
    rest = a - hi.astype(F32)
    mid = rest.astype(BF16)
    lo = (rest - mid.astype(F32)).astype(BF16)
    return hi, mid, lo


def mm(a, b, dims=NN):
    return lax.dot_general(a, b, dims, preferred_element_type=F32)


def exact(a, b, dims=NN):
    return lax.dot_general(a, b, dims, preferred_element_type=F32, precision=lax.Precision.HIGHEST)


def inverse_factor(gram):
    rows = lax.broadcasted_iota(jnp.int32, (RANK, 1), 0)
    eye = (lax.broadcasted_iota(jnp.int32, (RANK, RANK), 0) == lax.broadcasted_iota(jnp.int32, (RANK, RANK), 1)).astype(F32)
    left, right = gram, eye
    roots = jnp.zeros((RANK, 1), F32)
    for j in range(RANK):
        pivot = left[j : j + 1, j : j + 1]
        roots = jnp.where(rows == j, lax.rsqrt(pivot), roots)
        factor = jnp.where(rows > j, left[:, j : j + 1] / pivot, 0.0)
        left = left - factor * left[j : j + 1, :]
        right = right - factor * right[j : j + 1, :]
    return right * roots


def total_wait(ref, sem):
    pltpu.make_async_copy(ref, ref, sem).wait()


def send(ref, dst, send_sem, recv_sem, peer):
    pltpu.make_async_remote_copy(
        src_ref=ref, dst_ref=dst, send_sem=send_sem, recv_sem=recv_sem, device_id=peer, device_id_type=MESH
    ).start()


def loop(count, body):
    lax.fori_loop(0, count, lambda i, carry: (body(i), carry)[1], 0)


def exchange_kernel(
    g0, s0, e0, p0, g1, s1, e1, p1,
    columns, left, work,
    g_buf, e_buf, s_buf, p_buf, w_hi, w_lo,
    f_part, f_pair, f_z, f_all, gram_xy, inverse_ref, basis, summed,
    t_own, t_out, t_pair, t_xy, t_z,
    small_sems, in_sems, one_send, one_recv, fz_send, fz_recv, fp_send, fp_recv, tp_send, tp_recv,
    rs_send, rs_recv, tz_send, tz_recv, ag_send, ag_recv, cp_send, cp_recv,
):
    dp = lax.axis_index("dp")
    me = lax.axis_index("tensor")
    z, c = dp // 2, dp % 2
    x, y = me // 4, me % 4
    other = 1 - c
    sibling = {"dp": z * 2 + other, "tensor": me}

    def z_peer(i):
        return {"dp": lax.rem(z + 1 + lax.rem(i + 3, NZ - 1), NZ) * 2 + c, "tensor": me}

    def xy_index(i):
        k = 1 + lax.rem(i + 9, NXY - 1)
        return lax.rem(x + k // 4, 4) * 4 + lax.rem(y + k % 4, 4)

    def xy_peer(i):
        return {"dp": dp, "tensor": xy_index(i)}

    barrier = pltpu.get_barrier_semaphore()

    def greet(peer):
        pl.semaphore_signal(barrier, inc=1, device_id=peer, device_id_type=MESH)

    loop(NXY - 1, lambda i: greet(xy_peer(i)))
    loop(NZ - 1, lambda i: greet(z_peer(i)))
    greet(sibling)

    for m, (g, s, e, p) in enumerate(((g0, s0, e0, p0), (g1, s1, e1, p1))):
        pltpu.make_async_copy(s.at[0], s_buf.at[m], small_sems.at[m, 0]).start()
        pltpu.make_async_copy(p, p_buf.at[m], small_sems.at[m, 1]).start()

        def fetch(k):
            cols = pl.ds(pl.multiple_of(k * WIDTH, WIDTH), WIDTH)
            pltpu.make_async_copy(g.at[0, :, cols], g_buf.at[m, :, cols], in_sems.at[m, k, 0]).start()
            pltpu.make_async_copy(e.at[0, :, cols], e_buf.at[m, :, cols], in_sems.at[m, k, 1]).start()

        loop(CHUNKS, fetch)

    def partial(m):
        total_wait(s_buf.at[m], small_sems.at[m, 0])
        total_wait(p_buf.at[m], small_sems.at[m, 1])

        def chunk(k, total):
            cols = pl.ds(pl.multiple_of(k * WIDTH, WIDTH), WIDTH)
            total_wait(g_buf.at[m, :, cols], in_sems.at[m, k, 0])
            total_wait(e_buf.at[m, :, cols], in_sems.at[m, k, 1])
            count = WIDTH // BLOCK
            scale = s_buf[m, pl.ds(pl.multiple_of(k * count, count), count), :].T
            for b in range(count):
                at = pl.ds(pl.multiple_of(k * WIDTH + b * BLOCK, BLOCK), BLOCK)
                value = g_buf[m, :, at].astype(F32) * scale[:, b : b + 1] + e_buf[m, :, at].astype(F32)
                work[m, :, at] = value
                hi, lo = split2(value)
                w_hi[m, :, at] = hi
                w_lo[m, :, at] = lo
            prior = jnp.concatenate(split3(p_buf[m, :, cols]), 0)
            return total + mm(w_hi[m, :, cols], prior, NT) + mm(w_lo[m, :, cols], prior, NT)

        total = lax.fori_loop(0, CHUNKS, chunk, jnp.zeros((ROWS, 3 * RANK), F32))
        factor = total[:, :RANK] + (total[:, RANK : 2 * RANK] + total[:, 2 * RANK :])
        f_part[m] = factor.T

    loop(2, partial)
    summed[...] = jnp.zeros_like(summed)

    pl.semaphore_wait(barrier, 1 + (NZ - 1) + (NXY - 1))

    send(f_part.at[other], f_pair, one_send.at[0], one_recv.at[0], sibling)
    total_wait(f_pair, one_recv.at[0])
    for q in range(PARTS):
        rows = slice(q * RANKS, (q + 1) * RANKS)
        f_z[q, z] = f_part[c, rows] + f_pair[rows]

    def spread(q):
        loop(NZ - 1, lambda i: send(f_z.at[q, z], f_z.at[q, z], fz_send.at[q], fz_recv.at[q], z_peer(i)))

    loop(PARTS, spread)

    def terms(m, q):
        hi, lo = split2(f_all[m, q])
        lhs = jnp.concatenate([jnp.concatenate([hi, hi], 1), jnp.concatenate([lo, jnp.zeros_like(lo)], 1)], 0)
        both = mm(lhs, jnp.concatenate([w_hi[m], w_lo[m]], 0))
        return both[:RANKS] + both[RANKS:]

    def flow(i):
        @pl.when(i < PARTS)
        def _():
            q = i
            total_wait(f_z.at[q, pl.ds(0, NZ - 1)], fz_recv.at[q])
            total = f_z[q, 0]
            for k in range(1, NZ):
                total = total + f_z[q, k]
            f_all[c, q] = total
            send(f_all.at[c, q], f_all.at[c, q], fp_send.at[q], fp_recv.at[q], sibling)
            t_own[q] = terms(c, q)

        @pl.when((i >= 1) & (i < PARTS + 1))
        def _():
            q = i - 1
            total_wait(f_all.at[other, q], fp_recv.at[q])
            t_out[q] = terms(other, q)
            send(t_out.at[q], t_pair.at[q], tp_send.at[q], tp_recv.at[q], sibling)

        @pl.when(i >= 2)
        def _():
            q = i - 2
            total_wait(t_pair.at[q], tp_recv.at[q])
            t_own[q] = t_own[q] + t_pair[q]

            def scatter(j):
                cols = pl.ds(pl.multiple_of(xy_index(j) * PIECE, PIECE), PIECE)
                send(t_own.at[q, :, cols], t_xy.at[q, me], rs_send.at[q], rs_recv.at[q], xy_peer(j))

            loop(NXY - 1, scatter)
            t_xy[q, me] = t_own[q, :, pl.ds(pl.multiple_of(me * PIECE, PIECE), PIECE)]

    loop(PARTS + 2, flow)

    mine = jnp.concatenate([f_all[c, q] for q in range(PARTS)], 0)
    gram = exact(mine, mine, NT)
    gram_xy[me] = jnp.concatenate([gram[q * RANKS : (q + 1) * RANKS] for q in range(PARTS)], 1)
    loop(NXY - 1, lambda j: send(gram_xy.at[me], gram_xy.at[me], one_send.at[1], one_recv.at[1], xy_peer(j)))

    def middle(q):
        total_wait(t_xy.at[q, pl.ds(0, NXY - 1)], rs_recv.at[q])
        total = t_xy[q, 0]
        for k in range(1, NXY):
            total = total + t_xy[q, k]
        t_z[q, z] = total
        loop(NZ - 1, lambda i: send(t_z.at[q, z], t_z.at[q, z], tz_send.at[q], tz_recv.at[q], z_peer(i)))

    loop(PARTS, middle)

    total_wait(gram_xy.at[pl.ds(0, NXY - 1)], one_recv.at[1])
    packed = gram_xy[0]
    for k in range(1, NXY):
        packed = packed + gram_xy[k]
    gram = jnp.concatenate([packed[:, q * RANK : (q + 1) * RANK] for q in range(PARTS)], 0)
    inverse = inverse_factor(gram)
    basis[c] = exact(inverse, mine)
    send(basis.at[c], basis.at[c], one_send.at[2], one_recv.at[2], sibling)
    hi, mid, lo = split3(inverse)
    stacked = jnp.concatenate([hi, hi, mid, hi, mid, lo], 1)
    for q in range(PARTS):
        inverse_ref[q] = stacked[q * RANKS : (q + 1) * RANKS].astype(F32)

    own_cols = pl.ds(pl.multiple_of(me * PIECE, PIECE), PIECE)

    def gather(q):
        total_wait(t_z.at[q, pl.ds(0, NZ - 1)], tz_recv.at[q])
        total = t_z[q, 0]
        for k in range(1, NZ):
            total = total + t_z[q, k]
        rows = pl.ds(pl.multiple_of(q * RANKS, RANKS), RANKS)
        summed[rows, :] = total
        hi, mid, lo = split3(summed[...])
        rhs = jnp.concatenate([hi, mid, hi, lo, mid, hi], 0)
        columns[c, rows, own_cols] = mm(inverse_ref[q].astype(BF16), rhs) * (1.0 / 16.0)
        piece = columns.at[c, rows, own_cols]
        loop(NXY - 1, lambda j: send(piece, piece, ag_send.at[q], ag_recv.at[q], xy_peer(j)))

    loop(PARTS, gather)

    total_wait(basis.at[other], one_recv.at[2])
    for m in range(2):
        hi, lo = split2(basis[m].T)
        left[m] = jnp.concatenate([hi, hi, lo], 1)

    def hand(q):
        total_wait(t_xy.at[q, pl.ds(0, NXY - 1)], ag_recv.at[q])
        rows = pl.ds(pl.multiple_of(q * RANKS, RANKS), RANKS)
        send(columns.at[c, rows], columns.at[c, rows], cp_send.at[q], cp_recv.at[q], sibling)

    loop(PARTS, hand)

    def drain(q):
        rows = pl.ds(pl.multiple_of(q * RANKS, RANKS), RANKS)
        total_wait(columns.at[c, rows], cp_recv.at[q])
        total_wait(columns.at[c, rows], cp_send.at[q])
        total_wait(f_z.at[q, pl.ds(0, NZ - 1)], fz_send.at[q])
        total_wait(f_all.at[c, q], fp_send.at[q])
        total_wait(t_out.at[q], tp_send.at[q])
        total_wait(t_xy.at[q, pl.ds(0, NXY - 1)], rs_send.at[q])
        total_wait(t_z.at[q, pl.ds(0, NZ - 1)], tz_send.at[q])
        total_wait(t_xy.at[q, pl.ds(0, NXY - 1)], ag_send.at[q])

    loop(PARTS, drain)
    total_wait(f_pair, one_send.at[0])
    total_wait(gram_xy.at[pl.ds(0, NXY - 1)], one_send.at[1])
    total_wait(basis.at[c], one_send.at[2])


def exchange(*args):
    vmem, sems = pltpu.VMEM, pltpu.SemaphoreType.DMA
    return pl.pallas_call(
        exchange_kernel,
        out_shape=(
            jax.ShapeDtypeStruct((2, RANK, COLS), F32),
            jax.ShapeDtypeStruct((2, ROWS, 3 * RANK), BF16),
            jax.ShapeDtypeStruct((2, ROWS, COLS), F32),
        ),
        in_specs=[pl.BlockSpec(memory_space=pltpu.HBM)] * 8,
        out_specs=[pl.BlockSpec(memory_space=pltpu.VMEM)] * 3,
        scratch_shapes=[
            vmem((2, ROWS, COLS), BF16),
            vmem((2, ROWS, COLS), BF16),
            vmem((2, COLS // BLOCK, ROWS), F32),
            vmem((2, RANK, COLS), F32),
            vmem((2, ROWS, COLS), BF16),
            vmem((2, ROWS, COLS), BF16),
            vmem((2, RANK, ROWS), F32),
            vmem((RANK, ROWS), F32),
            vmem((PARTS, NZ, RANKS, ROWS), F32),
            vmem((2, PARTS, RANKS, ROWS), F32),
            vmem((NXY, RANKS, RANK * PARTS), F32),
            vmem((PARTS, RANKS, 6 * RANK), F32),
            vmem((2, RANK, ROWS), F32),
            vmem((RANK, PIECE), F32),
            vmem((PARTS, RANKS, COLS), F32),
            vmem((PARTS, RANKS, COLS), F32),
            vmem((PARTS, RANKS, COLS), F32),
            vmem((PARTS, NXY, RANKS, PIECE), F32),
            vmem((PARTS, NZ, RANKS, PIECE), F32),
            sems((2, 2)),
            sems((2, CHUNKS, 2)),
            sems((3,)),
            sems((3,)),
        ]
        + [sems((PARTS,))] * 14,
        compiler_params=pltpu.CompilerParams(collective_id=0, has_side_effects=True, vmem_limit_bytes=28 << 20),
        cost_estimate=pl.CostEstimate(flops=1 << 30, bytes_accessed=8 << 20, transcendentals=0),
    )(*args)


def finish_kernel(
    columns, left, work,
    out0, out1, update0, update1, residue0, residue1,
    update_buf, residue_buf, column_sems, out_sems,
):
    outs = (out0, out1)
    for m in range(2):
        pltpu.make_async_copy(columns.at[m], outs[m], column_sems.at[m]).start()
    for m, (update, residue) in enumerate(((update0, residue0), (update1, residue1))):

        def part(k):
            cols = pl.ds(pl.multiple_of(k * SLICE, SLICE), SLICE)
            hi, lo = split2(columns[m, :, cols])
            approx = mm(left[m], jnp.concatenate([hi, lo, hi], 0))
            update_buf[m, :, cols] = approx.astype(BF16)
            pltpu.make_async_copy(update_buf.at[m, :, cols], update.at[:, cols], out_sems.at[m, 0]).start()
            residue_buf[m, :, cols] = (work[m, :, cols] - approx).astype(BF16)
            pltpu.make_async_copy(residue_buf.at[m, :, cols], residue.at[0, :, cols], out_sems.at[m, 1]).start()

        loop(SLICES, part)
    for m in range(2):
        total_wait(columns.at[m], column_sems.at[m])
        total_wait(update_buf.at[m], out_sems.at[m, 0])
        total_wait(residue_buf.at[m], out_sems.at[m, 1])


def finish(columns, left, work):
    return pl.pallas_call(
        finish_kernel,
        out_shape=(
            jax.ShapeDtypeStruct((RANK, COLS), F32),
            jax.ShapeDtypeStruct((RANK, COLS), F32),
            jax.ShapeDtypeStruct((ROWS, COLS), BF16),
            jax.ShapeDtypeStruct((ROWS, COLS), BF16),
            jax.ShapeDtypeStruct((1, ROWS, COLS), BF16),
            jax.ShapeDtypeStruct((1, ROWS, COLS), BF16),
        ),
        in_specs=[pl.BlockSpec(memory_space=pltpu.VMEM)] * 3,
        out_specs=[pl.BlockSpec(memory_space=pltpu.HBM)] * 6,
        scratch_shapes=[
            pltpu.VMEM((2, ROWS, COLS), BF16),
            pltpu.VMEM((2, ROWS, COLS), BF16),
            pltpu.SemaphoreType.DMA((2,)),
            pltpu.SemaphoreType.DMA((2, 2)),
        ],
        compiler_params=pltpu.CompilerParams(vmem_limit_bytes=24 << 20),
    )(columns, left, work)


def shards(gate_grad, gate_scale, gate_error, gate_prior, up_grad, up_scale, up_error, up_prior):
    args = (
        gate_grad, gate_scale.transpose(0, 2, 1), gate_error, gate_prior.T,
        up_grad, up_scale.transpose(0, 2, 1), up_error, up_prior.T,
    )
    columns, left, work = exchange(*(pltpu.with_memory_space_constraint(a, pltpu.HBM) for a in args))
    columns0, columns1, update0, update1, residue0, residue1 = finish(columns, left, work)
    return (columns0.T, columns1.T, update0, update1, residue0, residue1)


def solution(mesh):
    in_specs = (
        P("dp", "tensor", None),
        P("dp", "tensor", None),
        P("dp", "tensor", None),
        P(),
        P("dp", "tensor", None),
        P("dp", "tensor", None),
        P("dp", "tensor", None),
        P(),
    )
    out_specs = (
        P(),
        P(),
        P("tensor", None),
        P("tensor", None),
        P("dp", "tensor", None),
        P("dp", "tensor", None),
    )
    return jax.shard_map(shards, mesh=mesh, in_specs=in_specs, out_specs=out_specs, check_vma=False)
```

time: 437 us -> 51.5 us (0.12)
  waiting for transfers between devices: 265 us -> 0 us
  blocking collectives: 110 us -> 0 us
  Pallas kernels: 0 us -> 50.7 us
  other arithmetic: 21.9 us -> 0 us
  matrix products: 17.8 us -> 0 us
  between operations: 14.2 us -> 0.64 us
  local copies, waits for them, and re-layouts: 7.96 us -> 0 us
    psum x1 -> x0, waiting for transfers between devices: 265 us -> none  [settle(): totals = lax.psum(terms, ('dp', 'tensor'))]
    psum x2 -> x0, blocking collectives: 110 us -> none  [the longest x1 60.7 us: settle(): grams = lax.psum(partial_gram, 'tensor')]
    pallas_call x0 -> x2, Pallas kernels: none -> 50.7 us  [the longest x1 47.1 us: exchange(): pl.pallas_call(exchange_kernel, out_shape=(jax.ShapeDtypeStruct((2, RANK,...]
    dot_general x8 -> x0, matrix products: 17.3 us -> none  [the longest x2 7.26 us: settle(): jnp.einsum('krd,krj->kdj', works, basis, precision=lax.Precision.HIGHEST)]
    another operation x10 -> x0, other arithmetic: 13.3 us -> none  [the longest x6 7.18 us: settle(): lower_factor = jnp.linalg.cholesky(grams)]
    mul x2 -> x0, local copies, waits for them, and re-layouts: 7.67 us -> none  [expand(): return (values * scale[..., None]).reshape(grad.shape)]
  transfers between devices with their start and end apart: 1 -> 0, of which waited for: 1 -> 0; matrix products, arithmetic and copies ran while one was open for 0% -> 0% of each run, Pallas kernels for 0% -> 0%
where the time goes in v2:
time: 51.5 us; the launch traced here: 51.3 us
  Pallas kernels  50.7 us (98%)
  between operations  0.64 us (1%)
    pallas_call x1, Pallas kernels, exchange(): pl.pallas_call(exchange_kernel, out_shape=(jax.ShapeDtypeStruct((2, RANK,...  47.1 us
    pallas_call x1, Pallas kernels, finish(): pl.pallas_call(finish_kernel, out_shape=(jax.ShapeDtypeStruct((RANK, COLS...  3.56 us

profile of v2, /device:TPU:1, one launch (start us, length us, event | category | flops | bytes accessed | tf_op | source)
XLA Modules:
  0.0 51.3 jit_solution(5416585599543778806)
XLA Ops:
  0.6 47.1 %shard_map.127 = (f32[2,32,4096]{2,1,0:T(8,128)S(1)}, bf16[2,128,96]{2,1,0:T(8,128)(2,1)S(1)}, f32[2,128,4096]{2,1,0:T(8,128)S(1)}) custom-call(bf16[1,128,4096]{2,1,0:T(8,128)(2,1)} %g0.1, f32[1,32,128]{2,1,0:T(8,128)} %bitcast.8, bf16[1,128,4096]{2,1,0:T(8,128)(2,1)} %e0.1, f32[32,4096]{1,0:T(8,128)} %bitcast.6, bf16[1,128,4096]{2,1,0:T(8,128)(2,1)} %g1.1, ...), custom_call_target="tpu_custom_call" | custom-call | flops 1073741824 | bytes 8388608 | tf_op jit(solution)/shard_map/pallas_call | solution.py:282
  47.8 3.6 %shard_map.128 = (f32[32,4096]{1,0:T(8,128)}, f32[32,4096]{1,0:T(8,128)}, bf16[128,4096]{1,0:T(8,128)(2,1)}, bf16[128,4096]{1,0:T(8,128)(2,1)}, bf16[1,128,4096]...) custom-call(f32[2,32,4096]{2,1,0:T(8,128)S(1)} %get-tuple-element.15.columns, ...), custom_call_target="tpu_custom_call" | custom-call | tf_op jit(solution)/shard_map/pallas_call | solution.py:349

commit v3 on v2

--- a/solution.py
+++ b/solution.py
@@ -20,6 +20,8 @@
 PIECE = COLS // NXY
 CHUNKS = 4
 WIDTH = COLS // CHUNKS
+LOADS = 2
+LOAD = COLS // LOADS
 SLICES = 8
 SLICE = COLS // SLICES
 
@@ -80,10 +82,10 @@
 def exchange_kernel(
     g0, s0, e0, p0, g1, s1, e1, p1,
     columns, left, work,
-    g_buf, e_buf, s_buf, p_buf, w_hi, w_lo,
+    g_buf, e_buf, s_buf, p_buf, w_pair, u_hi, u_lo,
     f_part, f_pair, f_z, f_all, gram_xy, inverse_ref, basis, summed,
-    t_own, t_out, t_pair, t_xy, t_z,
-    small_sems, in_sems, one_send, one_recv, fz_send, fz_recv, fp_send, fp_recv, tp_send, tp_recv,
+    t_own, t_xy, t_z,
+    small_sems, in_sems, one_send, one_recv, w_send, w_recv, fz_send, fz_recv,
     rs_send, rs_recv, tz_send, tz_recv, ag_send, ag_recv, cp_send, cp_recv,
 ):
     dp = lax.axis_index("dp")
@@ -103,6 +105,16 @@
     def xy_peer(i):
         return {"dp": dp, "tensor": xy_index(i)}
 
+    refs = ((g0, s0, e0, p0), (g1, s1, e1, p1))
+    for m, (g, sc, e, p) in enumerate(refs):
+        pltpu.make_async_copy(sc.at[0], s_buf.at[m], small_sems.at[m, 0]).start()
+        pltpu.make_async_copy(p, p_buf.at[m], small_sems.at[m, 1]).start()
+    for k in range(LOADS):
+        cols = pl.ds(k * LOAD, LOAD)
+        for m, (g, sc, e, p) in enumerate(refs):
+            pltpu.make_async_copy(g.at[0, :, cols], g_buf.at[m, :, cols], in_sems.at[m, k, 0]).start()
+            pltpu.make_async_copy(e.at[0, :, cols], e_buf.at[m, :, cols], in_sems.at[m, k, 1]).start()
+
     barrier = pltpu.get_barrier_semaphore()
 
     def greet(peer):
@@ -111,48 +123,63 @@
     loop(NXY - 1, lambda i: greet(xy_peer(i)))
     loop(NZ - 1, lambda i: greet(z_peer(i)))
     greet(sibling)
-
-    for m, (g, s, e, p) in enumerate(((g0, s0, e0, p0), (g1, s1, e1, p1))):
-        pltpu.make_async_copy(s.at[0], s_buf.at[m], small_sems.at[m, 0]).start()
-        pltpu.make_async_copy(p, p_buf.at[m], small_sems.at[m, 1]).start()
-
-        def fetch(k):
-            cols = pl.ds(pl.multiple_of(k * WIDTH, WIDTH), WIDTH)
-            pltpu.make_async_copy(g.at[0, :, cols], g_buf.at[m, :, cols], in_sems.at[m, k, 0]).start()
-            pltpu.make_async_copy(e.at[0, :, cols], e_buf.at[m, :, cols], in_sems.at[m, k, 1]).start()
-
-        loop(CHUNKS, fetch)
-
-    def partial(m):
+    summed[...] = jnp.zeros_like(summed)
+
+    for m in range(2):
         total_wait(s_buf.at[m], small_sems.at[m, 0])
         total_wait(p_buf.at[m], small_sems.at[m, 1])
 
-        def chunk(k, total):
-            cols = pl.ds(pl.multiple_of(k * WIDTH, WIDTH), WIDTH)
+    def partial(k, totals):
+        cols = pl.ds(pl.multiple_of(k * LOAD, LOAD), LOAD)
+        count = LOAD // BLOCK
+        for m in range(2):
             total_wait(g_buf.at[m, :, cols], in_sems.at[m, k, 0])
             total_wait(e_buf.at[m, :, cols], in_sems.at[m, k, 1])
-            count = WIDTH // BLOCK
+        result = []
+        zero = jnp.zeros((ROWS, BLOCK), BF16)
+        for m in range(2):
+            total = totals[m]
             scale = s_buf[m, pl.ds(pl.multiple_of(k * count, count), count), :].T
-            for b in range(count):
-                at = pl.ds(pl.multiple_of(k * WIDTH + b * BLOCK, BLOCK), BLOCK)
-                value = g_buf[m, :, at].astype(F32) * scale[:, b : b + 1] + e_buf[m, :, at].astype(F32)
-                work[m, :, at] = value
-                hi, lo = split2(value)
-                w_hi[m, :, at] = hi
-                w_lo[m, :, at] = lo
-            prior = jnp.concatenate(split3(p_buf[m, :, cols]), 0)
-            return total + mm(w_hi[m, :, cols], prior, NT) + mm(w_lo[m, :, cols], prior, NT)
-
-        total = lax.fori_loop(0, CHUNKS, chunk, jnp.zeros((ROWS, 3 * RANK), F32))
-        factor = total[:, :RANK] + (total[:, RANK : 2 * RANK] + total[:, 2 * RANK :])
+            for b in range(0, count, 2):
+                at = pl.ds(pl.multiple_of(k * LOAD + b * BLOCK, 2 * BLOCK), 2 * BLOCK)
+                hi, mid, lo = split3(p_buf[m, :, at])
+                prior = jnp.concatenate([hi, mid, lo, jnp.zeros_like(hi)], 0)
+                even = jnp.concatenate([prior[:, :BLOCK], zero], 1)
+                odd = jnp.concatenate([zero, prior[:, BLOCK:]], 1)
+                both = jnp.concatenate([g_buf[m, :, at], e_buf[m, :, at]], 0)
+                out = mm(both, jnp.concatenate([even, odd], 0), NT)
+                scaled = out[:ROWS, :128] * scale[:, b : b + 1] + out[:ROWS, 128:] * scale[:, b + 1 : b + 2]
+                total = total + (scaled + (out[ROWS:, :128] + out[ROWS:, 128:]))
+            result.append(total)
+        return tuple(result)
+
+    start = jnp.zeros((ROWS, 128), F32)
+    totals = lax.fori_loop(0, LOADS, partial, (start, start))
+    for m in range(2):
+        total = totals[m]
+        factor = total[:, :RANK] + (total[:, RANK : 2 * RANK] + total[:, 2 * RANK : 3 * RANK])
         f_part[m] = factor.T
 
-    loop(2, partial)
-    summed[...] = jnp.zeros_like(summed)
-
     pl.semaphore_wait(barrier, 1 + (NZ - 1) + (NXY - 1))
 
     send(f_part.at[other], f_pair, one_send.at[0], one_recv.at[0], sibling)
+
+    def values(m, k):
+        count = WIDTH // BLOCK
+        scale = s_buf[m, pl.ds(pl.multiple_of(k * count, count), count), :].T
+        for b in range(count):
+            at = pl.ds(pl.multiple_of(k * WIDTH + b * BLOCK, BLOCK), BLOCK)
+            work[m, :, at] = g_buf[m, :, at].astype(F32) * scale[:, b : b + 1] + e_buf[m, :, at].astype(F32)
+
+    def chunk_of(k):
+        return pl.ds(pl.multiple_of(k * WIDTH, WIDTH), WIDTH)
+
+    def give(k):
+        values(other, k)
+        cols = chunk_of(k)
+        send(work.at[other, :, cols], w_pair.at[:, cols], w_send.at[k], w_recv.at[k], sibling)
+
+    loop(CHUNKS, give)
     total_wait(f_pair, one_recv.at[0])
     for q in range(PARTS):
         rows = slice(q * RANKS, (q + 1) * RANKS)
@@ -163,47 +190,40 @@
 
     loop(PARTS, spread)
 
-    def terms(m, q):
-        hi, lo = split2(f_all[m, q])
+    loop(CHUNKS, lambda k: values(c, k))
+
+    def take(k):
+        cols = chunk_of(k)
+        total_wait(w_pair.at[:, cols], w_recv.at[k])
+        hi, lo = split2(work[c, :, cols] + w_pair[:, cols])
+        u_hi[:, cols] = hi
+        u_lo[:, cols] = lo
+
+    loop(CHUNKS, take)
+    total_wait(f_pair, one_send.at[0])
+    loop(CHUNKS, lambda k: total_wait(w_pair.at[:, chunk_of(k)], w_send.at[k]))
+
+    def flow(q):
+        total_wait(f_z.at[q, pl.ds(0, NZ - 1)], fz_recv.at[q])
+        total = f_z[q, 0]
+        for k in range(1, NZ):
+            total = total + f_z[q, k]
+        f_all[q] = total
+        hi, lo = split2(total)
         lhs = jnp.concatenate([jnp.concatenate([hi, hi], 1), jnp.concatenate([lo, jnp.zeros_like(lo)], 1)], 0)
-        both = mm(lhs, jnp.concatenate([w_hi[m], w_lo[m]], 0))
-        return both[:RANKS] + both[RANKS:]
-
-    def flow(i):
-        @pl.when(i < PARTS)
-        def _():
-            q = i
-            total_wait(f_z.at[q, pl.ds(0, NZ - 1)], fz_recv.at[q])
-            total = f_z[q, 0]
-            for k in range(1, NZ):
-                total = total + f_z[q, k]
-            f_all[c, q] = total
-            send(f_all.at[c, q], f_all.at[c, q], fp_send.at[q], fp_recv.at[q], sibling)
-            t_own[q] = terms(c, q)
-
-        @pl.when((i >= 1) & (i < PARTS + 1))
-        def _():
-            q = i - 1
-            total_wait(f_all.at[other, q], fp_recv.at[q])
-            t_out[q] = terms(other, q)
-            send(t_out.at[q], t_pair.at[q], tp_send.at[q], tp_recv.at[q], sibling)
-
-        @pl.when(i >= 2)
-        def _():
-            q = i - 2
-            total_wait(t_pair.at[q], tp_recv.at[q])
-            t_own[q] = t_own[q] + t_pair[q]
-
-            def scatter(j):
-                cols = pl.ds(pl.multiple_of(xy_index(j) * PIECE, PIECE), PIECE)
-                send(t_own.at[q, :, cols], t_xy.at[q, me], rs_send.at[q], rs_recv.at[q], xy_peer(j))
-
-            loop(NXY - 1, scatter)
-            t_xy[q, me] = t_own[q, :, pl.ds(pl.multiple_of(me * PIECE, PIECE), PIECE)]
-
-    loop(PARTS + 2, flow)
-
-    mine = jnp.concatenate([f_all[c, q] for q in range(PARTS)], 0)
+        both = mm(lhs, jnp.concatenate([u_hi[...], u_lo[...]], 0))
+        t_own[q] = both[:RANKS] + both[RANKS:]
+
+        def scatter(j):
+            cols = pl.ds(pl.multiple_of(xy_index(j) * PIECE, PIECE), PIECE)
+            send(t_own.at[q, :, cols], t_xy.at[q, me], rs_send.at[q], rs_recv.at[q], xy_peer(j))
+
+        loop(NXY - 1, scatter)
+        t_xy[q, me] = t_own[q, :, pl.ds(pl.multiple_of(me * PIECE, PIECE), PIECE)]
+
+    loop(PARTS, flow)
+
+    mine = jnp.concatenate([f_all[q] for q in range(PARTS)], 0)
     gram = exact(mine, mine, NT)
     gram_xy[me] = jnp.concatenate([gram[q * RANKS : (q + 1) * RANKS] for q in range(PARTS)], 1)
     loop(NXY - 1, lambda j: send(gram_xy.at[me], gram_xy.at[me], one_send.at[1], one_recv.at[1], xy_peer(j)))
@@ -217,6 +237,8 @@
         loop(NZ - 1, lambda i: send(t_z.at[q, z], t_z.at[q, z], tz_send.at[q], tz_recv.at[q], z_peer(i)))
 
     loop(PARTS, middle)
+    loop(PARTS, lambda q: total_wait(f_z.at[q, pl.ds(0, NZ - 1)], fz_send.at[q]))
+    loop(PARTS, lambda q: total_wait(t_xy.at[q, pl.ds(0, NXY - 1)], rs_send.at[q]))
 
     total_wait(gram_xy.at[pl.ds(0, NXY - 1)], one_recv.at[1])
     packed = gram_xy[0]
@@ -253,10 +275,15 @@
         hi, lo = split2(basis[m].T)
         left[m] = jnp.concatenate([hi, hi, lo], 1)
 
+    total_wait(gram_xy.at[pl.ds(0, NXY - 1)], one_send.at[1])
+    total_wait(basis.at[c], one_send.at[2])
+    loop(PARTS, lambda q: total_wait(t_z.at[q, pl.ds(0, NZ - 1)], tz_send.at[q]))
+
     def hand(q):
         total_wait(t_xy.at[q, pl.ds(0, NXY - 1)], ag_recv.at[q])
         rows = pl.ds(pl.multiple_of(q * RANKS, RANKS), RANKS)
         send(columns.at[c, rows], columns.at[c, rows], cp_send.at[q], cp_recv.at[q], sibling)
+        total_wait(t_xy.at[q, pl.ds(0, NXY - 1)], ag_send.at[q])
 
     loop(PARTS, hand)
 
@@ -264,17 +291,8 @@
         rows = pl.ds(pl.multiple_of(q * RANKS, RANKS), RANKS)
         total_wait(columns.at[c, rows], cp_recv.at[q])
         total_wait(columns.at[c, rows], cp_send.at[q])
-        total_wait(f_z.at[q, pl.ds(0, NZ - 1)], fz_send.at[q])
-        total_wait(f_all.at[c, q], fp_send.at[q])
-        total_wait(t_out.at[q], tp_send.at[q])
-        total_wait(t_xy.at[q, pl.ds(0, NXY - 1)], rs_send.at[q])
-        total_wait(t_z.at[q, pl.ds(0, NZ - 1)], tz_send.at[q])
-        total_wait(t_xy.at[q, pl.ds(0, NXY - 1)], ag_send.at[q])
 
     loop(PARTS, drain)
-    total_wait(f_pair, one_send.at[0])
-    total_wait(gram_xy.at[pl.ds(0, NXY - 1)], one_send.at[1])
-    total_wait(basis.at[c], one_send.at[2])
 
 
 def exchange(*args):
@@ -293,27 +311,28 @@
             vmem((2, ROWS, COLS), BF16),
             vmem((2, COLS // BLOCK, ROWS), F32),
             vmem((2, RANK, COLS), F32),
-            vmem((2, ROWS, COLS), BF16),
-            vmem((2, ROWS, COLS), BF16),
+            vmem((ROWS, COLS), F32),
+            vmem((ROWS, COLS), BF16),
+            vmem((ROWS, COLS), BF16),
             vmem((2, RANK, ROWS), F32),
             vmem((RANK, ROWS), F32),
             vmem((PARTS, NZ, RANKS, ROWS), F32),
-            vmem((2, PARTS, RANKS, ROWS), F32),
+            vmem((PARTS, RANKS, ROWS), F32),
             vmem((NXY, RANKS, RANK * PARTS), F32),
             vmem((PARTS, RANKS, 6 * RANK), F32),
             vmem((2, RANK, ROWS), F32),
             vmem((RANK, PIECE), F32),
             vmem((PARTS, RANKS, COLS), F32),
-            vmem((PARTS, RANKS, COLS), F32),
-            vmem((PARTS, RANKS, COLS), F32),
             vmem((PARTS, NXY, RANKS, PIECE), F32),
             vmem((PARTS, NZ, RANKS, PIECE), F32),
             sems((2, 2)),
-            sems((2, CHUNKS, 2)),
+            sems((2, LOADS, 2)),
             sems((3,)),
             sems((3,)),
+            sems((CHUNKS,)),
+            sems((CHUNKS,)),
         ]
-        + [sems((PARTS,))] * 14,
+        + [sems((PARTS,))] * 10,
         compiler_params=pltpu.CompilerParams(collective_id=0, has_side_effects=True, vmem_limit_bytes=28 << 20),
         cost_estimate=pl.CostEstimate(flops=1 << 30, bytes_accessed=8 << 20, transcendentals=0),
     )(*args)

time: 51.5 us -> 43.7 us (0.85)
  Pallas kernels: 50.7 us -> 42.9 us
    pallas_call x1, Pallas kernels: 47.1 us -> 39.4 us  [exchange(): pl.pallas_call(exchange_kernel, out_shape=(jax.ShapeDtypeStruct((2, RANK,...]
where the time goes in v3:
time: 43.7 us; the launch traced here: 43.6 us
  Pallas kernels  42.9 us (98%)
  between operations  0.64 us (1%)
    pallas_call x1, Pallas kernels, exchange(): pl.pallas_call(exchange_kernel, out_shape=(jax.ShapeDtypeStruct((2, RANK,...  39.4 us
    pallas_call x1, Pallas kernels, finish(): pl.pallas_call(finish_kernel, out_shape=(jax.ShapeDtypeStruct((RANK, COLS...  3.56 us

profile of v3, /device:TPU:1, one launch (start us, length us, event | category | flops | bytes accessed | tf_op | source)
XLA Modules:
  0.0 43.6 jit_solution(16032395538197201641)
XLA Ops:
  0.6 39.4 %shard_map.127 = (f32[2,32,4096]{2,1,0:T(8,128)S(1)}, bf16[2,128,96]{2,1,0:T(8,128)(2,1)S(1)}, f32[2,128,4096]{2,1,0:T(8,128)S(1)}) custom-call(bf16[1,128,4096]{2,1,0:T(8,128)(2,1)} %g0.1, f32[1,32,128]{2,1,0:T(8,128)} %bitcast.8, bf16[1,128,4096]{2,1,0:T(8,128)(2,1)} %e0.1, f32[32,4096]{1,0:T(8,128)} %bitcast.6, bf16[1,128,4096]{2,1,0:T(8,128)(2,1)} %g1.1, ...), custom_call_target="tpu_custom_call" | custom-call | flops 1073741824 | bytes 8388608 | tf_op jit(solution)/shard_map/pallas_call | solution.py:300
  40.0 3.6 %shard_map.128 = (f32[32,4096]{1,0:T(8,128)}, f32[32,4096]{1,0:T(8,128)}, bf16[128,4096]{1,0:T(8,128)(2,1)}, bf16[128,4096]{1,0:T(8,128)(2,1)}, bf16[1,128,4096]...) custom-call(f32[2,32,4096]{2,1,0:T(8,128)S(1)} %get-tuple-element.15.columns, ...), custom_call_target="tpu_custom_call" | custom-call | tf_op jit(solution)/shard_map/pallas_call | solution.py:368

commit v4 on v3

--- a/solution.py
+++ b/solution.py
@@ -22,7 +22,7 @@
 WIDTH = COLS // CHUNKS
 LOADS = 2
 LOAD = COLS // LOADS
-SLICES = 8
+SLICES = 4
 SLICE = COLS // SLICES
 
 NN = (((1,), (0,)), ((), ()))
@@ -76,17 +76,22 @@
 
 
 def loop(count, body):
+    if count in (NXY - 1, NZ - 1):
+        for i in range(count):
+            body(i)
+        return
+
     lax.fori_loop(0, count, lambda i, carry: (body(i), carry)[1], 0)
 
 
 def exchange_kernel(
     g0, s0, e0, p0, g1, s1, e1, p1,
-    columns, left, work,
+    sums, left, work,
     g_buf, e_buf, s_buf, p_buf, w_pair, u_hi, u_lo,
-    f_part, f_pair, f_z, f_all, gram_xy, inverse_ref, basis, summed,
+    f_part, f_pair, f_z, f_all, gram_xy, solved,
     t_own, t_xy, t_z,
     small_sems, in_sems, one_send, one_recv, w_send, w_recv, fz_send, fz_recv,
-    rs_send, rs_recv, tz_send, tz_recv, ag_send, ag_recv, cp_send, cp_recv,
+    rs_send, rs_recv, tz_send, tz_recv, ag_send, ag_recv, cp_send, cp_recv, last_send, last_recv,
 ):
     dp = lax.axis_index("dp")
     me = lax.axis_index("tensor")
@@ -96,14 +101,17 @@
     sibling = {"dp": z * 2 + other, "tensor": me}
 
     def z_peer(i):
-        return {"dp": lax.rem(z + 1 + lax.rem(i + 3, NZ - 1), NZ) * 2 + c, "tensor": me}
+        return {"dp": lax.rem(z + 1 + ((i + 3) % (NZ - 1)), NZ) * 2 + c, "tensor": me}
 
     def xy_index(i):
-        k = 1 + lax.rem(i + 9, NXY - 1)
+        k = 1 + ((i + 9) % (NXY - 1))
         return lax.rem(x + k // 4, 4) * 4 + lax.rem(y + k % 4, 4)
 
     def xy_peer(i):
         return {"dp": dp, "tensor": xy_index(i)}
+
+    def xy_cross(i):
+        return {"dp": z * 2 + other, "tensor": xy_index(i)}
 
     refs = ((g0, s0, e0, p0), (g1, s1, e1, p1))
     for m, (g, sc, e, p) in enumerate(refs):
@@ -122,8 +130,8 @@
 
     loop(NXY - 1, lambda i: greet(xy_peer(i)))
     loop(NZ - 1, lambda i: greet(z_peer(i)))
+    loop(NXY - 1, lambda i: greet(xy_cross(i)))
     greet(sibling)
-    summed[...] = jnp.zeros_like(summed)
 
     for m in range(2):
         total_wait(s_buf.at[m], small_sems.at[m, 0])
@@ -160,7 +168,7 @@
         factor = total[:, :RANK] + (total[:, RANK : 2 * RANK] + total[:, 2 * RANK : 3 * RANK])
         f_part[m] = factor.T
 
-    pl.semaphore_wait(barrier, 1 + (NZ - 1) + (NXY - 1))
+    pl.semaphore_wait(barrier, 1 + (NZ - 1) + 2 * (NXY - 1))
 
     send(f_part.at[other], f_pair, one_send.at[0], one_recv.at[0], sibling)
 
@@ -179,7 +187,7 @@
         cols = chunk_of(k)
         send(work.at[other, :, cols], w_pair.at[:, cols], w_send.at[k], w_recv.at[k], sibling)
 
-    loop(CHUNKS, give)
+    lax.fori_loop(0, CHUNKS // 2, lambda k, carry: (give(k), carry)[1], 0)
     total_wait(f_pair, one_recv.at[0])
     for q in range(PARTS):
         rows = slice(q * RANKS, (q + 1) * RANKS)
@@ -190,6 +198,7 @@
 
     loop(PARTS, spread)
 
+    lax.fori_loop(CHUNKS // 2, CHUNKS, lambda k, carry: (give(k), carry)[1], 0)
     loop(CHUNKS, lambda k: values(c, k))
 
     def take(k):
@@ -240,59 +249,70 @@
     loop(PARTS, lambda q: total_wait(f_z.at[q, pl.ds(0, NZ - 1)], fz_send.at[q]))
     loop(PARTS, lambda q: total_wait(t_xy.at[q, pl.ds(0, NXY - 1)], rs_send.at[q]))
 
+    own_cols = pl.ds(pl.multiple_of(me * PIECE, PIECE), PIECE)
+
+    def collect(q):
+        total_wait(t_z.at[q, pl.ds(0, NZ - 1)], tz_recv.at[q])
+        total = t_z[q, 0]
+        for k in range(1, NZ):
+            total = total + t_z[q, k]
+        rows = pl.ds(q * RANKS if isinstance(q, int) else pl.multiple_of(q * RANKS, RANKS), RANKS)
+        sums[c, rows, own_cols] = total
+        return sums.at[c, rows, own_cols]
+
+    def gather(q):
+        piece = collect(q)
+        loop(NXY - 1, lambda j: send(piece, piece, ag_send.at[q], ag_recv.at[q], xy_peer(j)))
+
+    loop(PARTS - 1, gather)
+    final = PARTS - 1
+    piece = collect(final)
+
+    def both_cores(j):
+        send(piece, piece, ag_send.at[final], ag_recv.at[final], xy_peer(j))
+        send(piece, piece, last_send.at[0], last_recv.at[0], xy_cross(j))
+
+    loop(NXY - 1, both_cores)
+    send(piece, piece, last_send.at[0], last_recv.at[0], sibling)
+
     total_wait(gram_xy.at[pl.ds(0, NXY - 1)], one_recv.at[1])
     packed = gram_xy[0]
     for k in range(1, NXY):
         packed = packed + gram_xy[k]
     gram = jnp.concatenate([packed[:, q * RANK : (q + 1) * RANK] for q in range(PARTS)], 0)
     inverse = inverse_factor(gram)
-    basis[c] = exact(inverse, mine)
-    send(basis.at[c], basis.at[c], one_send.at[2], one_recv.at[2], sibling)
-    hi, mid, lo = split3(inverse)
-    stacked = jnp.concatenate([hi, hi, mid, hi, mid, lo], 1)
-    for q in range(PARTS):
-        inverse_ref[q] = stacked[q * RANKS : (q + 1) * RANKS].astype(F32)
-
-    own_cols = pl.ds(pl.multiple_of(me * PIECE, PIECE), PIECE)
-
-    def gather(q):
-        total_wait(t_z.at[q, pl.ds(0, NZ - 1)], tz_recv.at[q])
-        total = t_z[q, 0]
-        for k in range(1, NZ):
-            total = total + t_z[q, k]
-        rows = pl.ds(pl.multiple_of(q * RANKS, RANKS), RANKS)
-        summed[rows, :] = total
-        hi, mid, lo = split3(summed[...])
-        rhs = jnp.concatenate([hi, mid, hi, lo, mid, hi], 0)
-        columns[c, rows, own_cols] = mm(inverse_ref[q].astype(BF16), rhs) * (1.0 / 16.0)
-        piece = columns.at[c, rows, own_cols]
-        loop(NXY - 1, lambda j: send(piece, piece, ag_send.at[q], ag_recv.at[q], xy_peer(j)))
-
-    loop(PARTS, gather)
-
-    total_wait(basis.at[other], one_recv.at[2])
-    for m in range(2):
-        hi, lo = split2(basis[m].T)
-        left[m] = jnp.concatenate([hi, hi, lo], 1)
-
-    total_wait(gram_xy.at[pl.ds(0, NXY - 1)], one_send.at[1])
-    total_wait(basis.at[c], one_send.at[2])
-    loop(PARTS, lambda q: total_wait(t_z.at[q, pl.ds(0, NZ - 1)], tz_send.at[q]))
+    basis = exact(inverse, mine)
+    solved[c, 0] = exact(inverse.T, basis)
+    solved[c, 1] = jnp.concatenate([inverse.T, jnp.zeros((RANK, ROWS - RANK), F32)], 1)
+    send(solved.at[c], solved.at[c], one_send.at[2], one_recv.at[2], sibling)
 
     def hand(q):
         total_wait(t_xy.at[q, pl.ds(0, NXY - 1)], ag_recv.at[q])
         rows = pl.ds(pl.multiple_of(q * RANKS, RANKS), RANKS)
-        send(columns.at[c, rows], columns.at[c, rows], cp_send.at[q], cp_recv.at[q], sibling)
-        total_wait(t_xy.at[q, pl.ds(0, NXY - 1)], ag_send.at[q])
-
-    loop(PARTS, hand)
+        send(sums.at[c, rows], sums.at[c, rows], cp_send.at[q], cp_recv.at[q], sibling)
+
+    loop(PARTS - 1, hand)
+
+    total_wait(solved.at[other], one_recv.at[2])
+    for m in range(2):
+        both = jnp.concatenate([solved[m, 0].T, solved[m, 1].T[:RANK]], 0) * (1.0 / 16.0)
+        hi, mid, lo = split3(both)
+        left[m] = jnp.concatenate([hi, hi, mid, hi, mid, lo], 1)
+
+    total_wait(gram_xy.at[pl.ds(0, NXY - 1)], one_send.at[1])
+    total_wait(solved.at[c], one_send.at[2])
+    loop(PARTS, lambda q: total_wait(t_z.at[q, pl.ds(0, NZ - 1)], tz_send.at[q]))
 
     def drain(q):
         rows = pl.ds(pl.multiple_of(q * RANKS, RANKS), RANKS)
-        total_wait(columns.at[c, rows], cp_recv.at[q])
-        total_wait(columns.at[c, rows], cp_send.at[q])
-
-    loop(PARTS, drain)
+        total_wait(sums.at[c, rows], cp_recv.at[q])
+        total_wait(sums.at[c, rows], cp_send.at[q])
+
+    loop(PARTS - 1, drain)
+    loop(PARTS, lambda q: total_wait(t_xy.at[q, pl.ds(0, NXY - 1)], ag_send.at[q]))
+    total_wait(t_xy.at[0], last_send.at[0])
+    total_wait(t_xy.at[0, pl.ds(0, NXY - 1)], ag_recv.at[final])
+    total_wait(t_xy.at[0], last_recv.at[0])
 
 
 def exchange(*args):
@@ -301,7 +321,7 @@
         exchange_kernel,
         out_shape=(
             jax.ShapeDtypeStruct((2, RANK, COLS), F32),
-            jax.ShapeDtypeStruct((2, ROWS, 3 * RANK), BF16),
+            jax.ShapeDtypeStruct((2, ROWS + RANK, 6 * RANK), BF16),
             jax.ShapeDtypeStruct((2, ROWS, COLS), F32),
         ),
         in_specs=[pl.BlockSpec(memory_space=pltpu.HBM)] * 8,
@@ -319,9 +339,7 @@
             vmem((PARTS, NZ, RANKS, ROWS), F32),
             vmem((PARTS, RANKS, ROWS), F32),
             vmem((NXY, RANKS, RANK * PARTS), F32),
-            vmem((PARTS, RANKS, 6 * RANK), F32),
-            vmem((2, RANK, ROWS), F32),
-            vmem((RANK, PIECE), F32),
+            vmem((2, 2, RANK, ROWS), F32),
             vmem((PARTS, RANKS, COLS), F32),
             vmem((PARTS, NXY, RANKS, PIECE), F32),
             vmem((PARTS, NZ, RANKS, PIECE), F32),
@@ -332,39 +350,41 @@
             sems((CHUNKS,)),
             sems((CHUNKS,)),
         ]
-        + [sems((PARTS,))] * 10,
+        + [sems((PARTS,))] * 10
+        + [sems((1,))] * 2,
         compiler_params=pltpu.CompilerParams(collective_id=0, has_side_effects=True, vmem_limit_bytes=28 << 20),
         cost_estimate=pl.CostEstimate(flops=1 << 30, bytes_accessed=8 << 20, transcendentals=0),
     )(*args)
 
 
 def finish_kernel(
-    columns, left, work,
+    sums, left, work,
     out0, out1, update0, update1, residue0, residue1,
-    update_buf, residue_buf, column_sems, out_sems,
+    out_buf, update_buf, residue_buf, out_sems,
 ):
-    outs = (out0, out1)
+    outputs = ((out0, update0, residue0), (out1, update1, residue1))
+
+    def part(k):
+        cols = pl.ds(pl.multiple_of(k * SLICE, SLICE), SLICE)
+        for m, (out, update, residue) in enumerate(outputs):
+            hi, mid, lo = split3(sums[m, :, cols])
+            both = mm(left[m], jnp.concatenate([hi, mid, hi, lo, mid, hi], 0))
+            approx = both[:ROWS]
+            update_buf[m, :, cols] = approx.astype(BF16)
+            residue_buf[m, :, cols] = (work[m, :, cols] - approx).astype(BF16)
+            out_buf[m, :, cols] = both[ROWS:]
+            pltpu.make_async_copy(update_buf.at[m, :, cols], update.at[:, cols], out_sems.at[m, 0]).start()
+            pltpu.make_async_copy(residue_buf.at[m, :, cols], residue.at[0, :, cols], out_sems.at[m, 1]).start()
+            pltpu.make_async_copy(out_buf.at[m, :, cols], out.at[:, cols], out_sems.at[m, 2]).start()
+
+    loop(SLICES, part)
     for m in range(2):
-        pltpu.make_async_copy(columns.at[m], outs[m], column_sems.at[m]).start()
-    for m, (update, residue) in enumerate(((update0, residue0), (update1, residue1))):
-
-        def part(k):
-            cols = pl.ds(pl.multiple_of(k * SLICE, SLICE), SLICE)
-            hi, lo = split2(columns[m, :, cols])
-            approx = mm(left[m], jnp.concatenate([hi, lo, hi], 0))
-            update_buf[m, :, cols] = approx.astype(BF16)
-            pltpu.make_async_copy(update_buf.at[m, :, cols], update.at[:, cols], out_sems.at[m, 0]).start()
-            residue_buf[m, :, cols] = (work[m, :, cols] - approx).astype(BF16)
-            pltpu.make_async_copy(residue_buf.at[m, :, cols], residue.at[0, :, cols], out_sems.at[m, 1]).start()
-
-        loop(SLICES, part)
-    for m in range(2):
-        total_wait(columns.at[m], column_sems.at[m])
         total_wait(update_buf.at[m], out_sems.at[m, 0])
         total_wait(residue_buf.at[m], out_sems.at[m, 1])
-
-
-def finish(columns, left, work):
+        total_wait(out_buf.at[m], out_sems.at[m, 2])
+
+
+def finish(sums, left, work):
     return pl.pallas_call(
         finish_kernel,
         out_shape=(
@@ -378,13 +398,13 @@
         in_specs=[pl.BlockSpec(memory_space=pltpu.VMEM)] * 3,
         out_specs=[pl.BlockSpec(memory_space=pltpu.HBM)] * 6,
         scratch_shapes=[
+            pltpu.VMEM((2, RANK, COLS), F32),
             pltpu.VMEM((2, ROWS, COLS), BF16),
             pltpu.VMEM((2, ROWS, COLS), BF16),
-            pltpu.SemaphoreType.DMA((2,)),
-            pltpu.SemaphoreType.DMA((2, 2)),
+            pltpu.SemaphoreType.DMA((2, 3)),
         ],
         compiler_params=pltpu.CompilerParams(vmem_limit_bytes=24 << 20),
-    )(columns, left, work)
+    )(sums, left, work)
 
 
 def shards(gate_grad, gate_scale, gate_error, gate_prior, up_grad, up_scale, up_error, up_prior):
@@ -392,8 +412,8 @@
         gate_grad, gate_scale.transpose(0, 2, 1), gate_error, gate_prior.T,
         up_grad, up_scale.transpose(0, 2, 1), up_error, up_prior.T,
     )
-    columns, left, work = exchange(*(pltpu.with_memory_space_constraint(a, pltpu.HBM) for a in args))
-    columns0, columns1, update0, update1, residue0, residue1 = finish(columns, left, work)
+    sums, left, work = exchange(*(pltpu.with_memory_space_constraint(a, pltpu.HBM) for a in args))
+    columns0, columns1, update0, update1, residue0, residue1 = finish(sums, left, work)
     return (columns0.T, columns1.T, update0, update1, residue0, residue1)
 
 

time: 43.7 us -> 40.8 us (0.934)
  Pallas kernels: 42.9 us -> 40.1 us
    pallas_call x1, Pallas kernels: 39.4 us -> 37.5 us  [exchange(): pl.pallas_call(exchange_kernel, out_shape=(jax.ShapeDtypeStruct((2, RANK,...]
    pallas_call x1, Pallas kernels: 3.56 us -> 2.6 us  [finish(): pl.pallas_call(finish_kernel, out_shape=(jax.ShapeDtypeStruct((RANK, COLS...]
where the time goes in v4:
time: 40.8 us; the launch traced here: 40.7 us
  Pallas kernels  40.1 us (98%)
  between operations  0.64 us (2%)
    pallas_call x1, Pallas kernels, exchange(): pl.pallas_call(exchange_kernel, out_shape=(jax.ShapeDtypeStruct((2, RANK,...  37.5 us
    pallas_call x1, Pallas kernels, finish(): pl.pallas_call(finish_kernel, out_shape=(jax.ShapeDtypeStruct((RANK, COLS...  2.6 us

profile of v4, /device:TPU:1, one launch (start us, length us, event | category | flops | bytes accessed | tf_op | source)
XLA Modules:
  0.0 40.7 jit_solution(4356318837749736044)
XLA Ops:
  0.6 37.5 %shard_map.127 = (f32[2,32,4096]{2,1,0:T(8,128)S(1)}, bf16[2,160,192]{2,1,0:T(8,128)(2,1)S(1)}, f32[2,128,4096]{2,1,0:T(8,128)S(1)}) custom-call(bf16[1,128,4096]{2,1,0:T(8,128)(2,1)} %g0.1, f32[1,32,128]{2,1,0:T(8,128)} %bitcast.8, bf16[1,128,4096]{2,1,0:T(8,128)(2,1)} %e0.1, f32[32,4096]{1,0:T(8,128)} %bitcast.6, bf16[1,128,4096]{2,1,0:T(8,128)(2,1)} %g1.1, ...), custom_call_target="tpu_custom_call" | custom-call | flops 1073741824 | bytes 8388608 | tf_op jit(solution)/shard_map/pallas_call | solution.py:320
  38.1 2.6 %shard_map.128 = (f32[32,4096]{1,0:T(8,128)}, f32[32,4096]{1,0:T(8,128)}, bf16[128,4096]{1,0:T(8,128)(2,1)}, bf16[128,4096]{1,0:T(8,128)(2,1)}, bf16[1,128,4096]...) custom-call(f32[2,32,4096]{2,1,0:T(8,128)S(1)} %get-tuple-element.15.sums, bf16[2,160,192]{2,1,0:T(8,128)(2,1)S(1)} %get-tuple-element.16.left, ...), custom_call_target="tpu_custom_call" | custom-call | tf_op jit(solution)/shard_map/pallas_call | solution.py:388

commit v5 on v4

--- a/solution.py
+++ b/solution.py
@@ -18,12 +18,17 @@
 PARTS = 4
 RANKS = RANK // PARTS
 PIECE = COLS // NXY
+HALF = PIECE // 2
+UNITS = ((0, 0, PIECE), (1, 0, PIECE), (2, 0, PIECE), (3, 0, PIECE))
 CHUNKS = 4
 WIDTH = COLS // CHUNKS
 LOADS = 2
 LOAD = COLS // LOADS
-SLICES = 4
+SLICES = 8
 SLICE = COLS // SLICES
+
+FAR_Z = (4, 3, 5, 2, 6, 1, 7)
+FAR_XY = (10, 6, 14, 9, 11, 5, 7, 13, 15, 2, 8, 1, 3, 4, 12)
 
 NN = (((1,), (0,)), ((), ()))
 NT = (((1,), (1,)), ((), ()))
@@ -75,12 +80,16 @@
     ).start()
 
 
-def loop(count, body):
-    if count in (NXY - 1, NZ - 1):
+def loop(count, body, unroll=False):
+    if count in (NXY - 1, NZ - 1, NZ):
         for i in range(count):
             body(i)
         return
 
+    if unroll:
+        for i in range(count):
+            body(i)
+        return
     lax.fori_loop(0, count, lambda i, carry: (body(i), carry)[1], 0)
 
 
@@ -100,12 +109,17 @@
     other = 1 - c
     sibling = {"dp": z * 2 + other, "tensor": me}
 
+    z_bases = [lax.rem(z + k, NZ) * 2 for k in FAR_Z + (0,)]
+    xy_all = [lax.rem(x + k // 4, 4) * 4 + lax.rem(y + k % 4, 4) for k in FAR_XY]
+
     def z_peer(i):
-        return {"dp": lax.rem(z + 1 + ((i + 3) % (NZ - 1)), NZ) * 2 + c, "tensor": me}
+        return {"dp": z_bases[i] + c, "tensor": me}
+
+    def z_cross(i):
+        return {"dp": z_bases[i] + other, "tensor": me}
 
     def xy_index(i):
-        k = 1 + ((i + 9) % (NXY - 1))
-        return lax.rem(x + k // 4, 4) * 4 + lax.rem(y + k % 4, 4)
+        return xy_all[i]
 
     def xy_peer(i):
         return {"dp": dp, "tensor": xy_index(i)}
@@ -117,21 +131,24 @@
     for m, (g, sc, e, p) in enumerate(refs):
         pltpu.make_async_copy(sc.at[0], s_buf.at[m], small_sems.at[m, 0]).start()
         pltpu.make_async_copy(p, p_buf.at[m], small_sems.at[m, 1]).start()
-    for k in range(LOADS):
+
+    def fetch(k):
         cols = pl.ds(k * LOAD, LOAD)
         for m, (g, sc, e, p) in enumerate(refs):
             pltpu.make_async_copy(g.at[0, :, cols], g_buf.at[m, :, cols], in_sems.at[m, k, 0]).start()
             pltpu.make_async_copy(e.at[0, :, cols], e_buf.at[m, :, cols], in_sems.at[m, k, 1]).start()
 
+    fetch(0)
     barrier = pltpu.get_barrier_semaphore()
 
     def greet(peer):
         pl.semaphore_signal(barrier, inc=1, device_id=peer, device_id_type=MESH)
 
+    loop(NZ - 1, lambda i: greet(z_peer(i)))
+    greet(sibling)
     loop(NXY - 1, lambda i: greet(xy_peer(i)))
-    loop(NZ - 1, lambda i: greet(z_peer(i)))
-    loop(NXY - 1, lambda i: greet(xy_cross(i)))
-    greet(sibling)
+    for k in range(1, LOADS):
+        fetch(k)
 
     for m in range(2):
         total_wait(s_buf.at[m], small_sems.at[m, 0])
@@ -168,9 +185,13 @@
         factor = total[:, :RANK] + (total[:, RANK : 2 * RANK] + total[:, 2 * RANK : 3 * RANK])
         f_part[m] = factor.T
 
-    pl.semaphore_wait(barrier, 1 + (NZ - 1) + 2 * (NXY - 1))
+    pl.semaphore_wait(barrier, NZ + (NXY - 1))
 
     send(f_part.at[other], f_pair, one_send.at[0], one_recv.at[0], sibling)
+
+    def spread(q):
+        f_z[q, z] = f_part[c, q * RANKS : (q + 1) * RANKS] + f_pair[q * RANKS : (q + 1) * RANKS]
+        loop(NZ - 1, lambda i: send(f_z.at[q, z], f_z.at[q, z], fz_send.at[q], fz_recv.at[q], z_peer(i)))
 
     def values(m, k):
         count = WIDTH // BLOCK
@@ -187,18 +208,13 @@
         cols = chunk_of(k)
         send(work.at[other, :, cols], w_pair.at[:, cols], w_send.at[k], w_recv.at[k], sibling)
 
-    lax.fori_loop(0, CHUNKS // 2, lambda k, carry: (give(k), carry)[1], 0)
+    give(0)
+    give(1)
     total_wait(f_pair, one_recv.at[0])
     for q in range(PARTS):
-        rows = slice(q * RANKS, (q + 1) * RANKS)
-        f_z[q, z] = f_part[c, rows] + f_pair[rows]
-
-    def spread(q):
-        loop(NZ - 1, lambda i: send(f_z.at[q, z], f_z.at[q, z], fz_send.at[q], fz_recv.at[q], z_peer(i)))
-
-    loop(PARTS, spread)
-
-    lax.fori_loop(CHUNKS // 2, CHUNKS, lambda k, carry: (give(k), carry)[1], 0)
+        spread(q)
+    lax.fori_loop(2, CHUNKS, lambda k, carry: (give(k), carry)[1], 0)
+
     loop(CHUNKS, lambda k: values(c, k))
 
     def take(k):
@@ -223,14 +239,14 @@
         both = mm(lhs, jnp.concatenate([u_hi[...], u_lo[...]], 0))
         t_own[q] = both[:RANKS] + both[RANKS:]
 
-        def scatter(j):
-            cols = pl.ds(pl.multiple_of(xy_index(j) * PIECE, PIECE), PIECE)
-            send(t_own.at[q, :, cols], t_xy.at[q, me], rs_send.at[q], rs_recv.at[q], xy_peer(j))
-
-        loop(NXY - 1, scatter)
-        t_xy[q, me] = t_own[q, :, pl.ds(pl.multiple_of(me * PIECE, PIECE), PIECE)]
-
-    loop(PARTS, flow)
+        for u, (chunk, first, width) in enumerate(UNITS):
+            if chunk == q:
+                for j in range(NXY - 1):
+                    cols = pl.ds(pl.multiple_of(first + xy_index(j) * width, width), width)
+                    send(t_own.at[q, :, cols], t_xy.at[u, me, :, :width], rs_send.at[u], rs_recv.at[u], xy_peer(j))
+                t_xy[u, me, :, :width] = t_own[q, :, pl.ds(pl.multiple_of(first + me * width, width), width)]
+
+    loop(PARTS, flow, True)
 
     mine = jnp.concatenate([f_all[q] for q in range(PARTS)], 0)
     gram = exact(mine, mine, NT)
@@ -238,34 +254,37 @@
     loop(NXY - 1, lambda j: send(gram_xy.at[me], gram_xy.at[me], one_send.at[1], one_recv.at[1], xy_peer(j)))
 
     def middle(q):
-        total_wait(t_xy.at[q, pl.ds(0, NXY - 1)], rs_recv.at[q])
-        total = t_xy[q, 0]
+        width = UNITS[q][2]
+        total_wait(t_xy.at[q, pl.ds(0, NXY - 1), :, :width], rs_recv.at[q])
+        total = t_xy[q, 0, :, :width]
         for k in range(1, NXY):
-            total = total + t_xy[q, k]
-        t_z[q, z] = total
-        loop(NZ - 1, lambda i: send(t_z.at[q, z], t_z.at[q, z], tz_send.at[q], tz_recv.at[q], z_peer(i)))
-
-    loop(PARTS, middle)
+            total = total + t_xy[q, k, :, :width]
+        t_z[q, z, :, :width] = total
+        piece = t_z.at[q, z, :, :width]
+        loop(NZ - 1, lambda i: send(piece, piece, tz_send.at[q], tz_recv.at[q], z_peer(i)))
+
+    loop(len(UNITS), middle, True)
     loop(PARTS, lambda q: total_wait(f_z.at[q, pl.ds(0, NZ - 1)], fz_send.at[q]))
-    loop(PARTS, lambda q: total_wait(t_xy.at[q, pl.ds(0, NXY - 1)], rs_send.at[q]))
-
-    own_cols = pl.ds(pl.multiple_of(me * PIECE, PIECE), PIECE)
-
-    def collect(q):
-        total_wait(t_z.at[q, pl.ds(0, NZ - 1)], tz_recv.at[q])
-        total = t_z[q, 0]
+    for u, (chunk, first, width) in enumerate(UNITS):
+        total_wait(t_xy.at[u, pl.ds(0, NXY - 1), :, :width], rs_send.at[u])
+
+    def collect(u):
+        chunk, first, width = UNITS[u]
+        total_wait(t_z.at[u, pl.ds(0, NZ - 1), :, :width], tz_recv.at[u])
+        total = t_z[u, 0, :, :width]
         for k in range(1, NZ):
-            total = total + t_z[q, k]
-        rows = pl.ds(q * RANKS if isinstance(q, int) else pl.multiple_of(q * RANKS, RANKS), RANKS)
-        sums[c, rows, own_cols] = total
-        return sums.at[c, rows, own_cols]
-
-    def gather(q):
-        piece = collect(q)
-        loop(NXY - 1, lambda j: send(piece, piece, ag_send.at[q], ag_recv.at[q], xy_peer(j)))
-
-    loop(PARTS - 1, gather)
-    final = PARTS - 1
+            total = total + t_z[u, k, :, :width]
+        rows = pl.ds(chunk * RANKS, RANKS)
+        cols = pl.ds(pl.multiple_of(first + me * width, width), width)
+        sums[c, rows, cols] = total
+        return sums.at[c, rows, cols]
+
+    def gather(u):
+        piece = collect(u)
+        loop(NXY - 1, lambda j: send(piece, piece, ag_send.at[u], ag_recv.at[u], xy_peer(j)))
+
+    final = len(UNITS) - 1
+    loop(final, gather, True)
     piece = collect(final)
 
     def both_cores(j):
@@ -286,12 +305,15 @@
     solved[c, 1] = jnp.concatenate([inverse.T, jnp.zeros((RANK, ROWS - RANK), F32)], 1)
     send(solved.at[c], solved.at[c], one_send.at[2], one_recv.at[2], sibling)
 
-    def hand(q):
-        total_wait(t_xy.at[q, pl.ds(0, NXY - 1)], ag_recv.at[q])
-        rows = pl.ds(pl.multiple_of(q * RANKS, RANKS), RANKS)
-        send(sums.at[c, rows], sums.at[c, rows], cp_send.at[q], cp_recv.at[q], sibling)
-
-    loop(PARTS - 1, hand)
+    def part_of(u):
+        chunk, first, width = UNITS[u]
+        return sums.at[c, pl.ds(chunk * RANKS, RANKS), pl.ds(first, width * NXY)]
+
+    def hand(u):
+        total_wait(t_xy.at[u, pl.ds(0, NXY - 1), :, : UNITS[u][2]], ag_recv.at[u])
+        send(part_of(u), part_of(u), cp_send.at[u], cp_recv.at[u], sibling)
+
+    loop(final, hand, True)
 
     total_wait(solved.at[other], one_recv.at[2])
     for m in range(2):
@@ -301,18 +323,15 @@
 
     total_wait(gram_xy.at[pl.ds(0, NXY - 1)], one_send.at[1])
     total_wait(solved.at[c], one_send.at[2])
-    loop(PARTS, lambda q: total_wait(t_z.at[q, pl.ds(0, NZ - 1)], tz_send.at[q]))
-
-    def drain(q):
-        rows = pl.ds(pl.multiple_of(q * RANKS, RANKS), RANKS)
-        total_wait(sums.at[c, rows], cp_recv.at[q])
-        total_wait(sums.at[c, rows], cp_send.at[q])
-
-    loop(PARTS - 1, drain)
-    loop(PARTS, lambda q: total_wait(t_xy.at[q, pl.ds(0, NXY - 1)], ag_send.at[q]))
-    total_wait(t_xy.at[0], last_send.at[0])
-    total_wait(t_xy.at[0, pl.ds(0, NXY - 1)], ag_recv.at[final])
-    total_wait(t_xy.at[0], last_recv.at[0])
+    for u, (chunk, first, width) in enumerate(UNITS):
+        total_wait(t_z.at[u, pl.ds(0, NZ - 1), :, :width], tz_send.at[u])
+        total_wait(t_xy.at[u, pl.ds(0, NXY - 1), :, :width], ag_send.at[u])
+    total_wait(t_xy.at[0, :, :, : UNITS[final][2]], last_send.at[0])
+    for u in range(final):
+        total_wait(part_of(u), cp_recv.at[u])
+        total_wait(part_of(u), cp_send.at[u])
+    total_wait(t_xy.at[0, pl.ds(0, NXY - 1), :, : UNITS[final][2]], ag_recv.at[final])
+    total_wait(t_xy.at[0, :, :, : UNITS[final][2]], last_recv.at[0])
 
 
 def exchange(*args):
@@ -341,8 +360,8 @@
             vmem((NXY, RANKS, RANK * PARTS), F32),
             vmem((2, 2, RANK, ROWS), F32),
             vmem((PARTS, RANKS, COLS), F32),
-            vmem((PARTS, NXY, RANKS, PIECE), F32),
-            vmem((PARTS, NZ, RANKS, PIECE), F32),
+            vmem((len(UNITS), NXY, RANKS, PIECE), F32),
+            vmem((len(UNITS), NZ, RANKS, PIECE), F32),
             sems((2, 2)),
             sems((2, LOADS, 2)),
             sems((3,)),
@@ -350,7 +369,7 @@
             sems((CHUNKS,)),
             sems((CHUNKS,)),
         ]
-        + [sems((PARTS,))] * 10
+        + [sems((len(UNITS),))] * 10
         + [sems((1,))] * 2,
         compiler_params=pltpu.CompilerParams(collective_id=0, has_side_effects=True, vmem_limit_bytes=28 << 20),
         cost_estimate=pl.CostEstimate(flops=1 << 30, bytes_accessed=8 << 20, transcendentals=0),

time: 40.8 us -> 39.6 us (0.971)
  Pallas kernels: 40.1 us -> 38.8 us
    pallas_call x1, Pallas kernels: 37.5 us -> 36.2 us  [exchange(): pl.pallas_call(exchange_kernel, out_shape=(jax.ShapeDtypeStruct((2, RANK,...]
where the time goes in v5:
time: 39.6 us; the launch traced here: 39.4 us
  Pallas kernels  38.8 us (98%)
  between operations  0.64 us (2%)
    pallas_call x1, Pallas kernels, exchange(): pl.pallas_call(exchange_kernel, out_shape=(jax.ShapeDtypeStruct((2, RANK,...  36.2 us
    pallas_call x1, Pallas kernels, finish(): pl.pallas_call(finish_kernel, out_shape=(jax.ShapeDtypeStruct((RANK, COLS...  2.54 us

profile of v5, /device:TPU:1, one launch (start us, length us, event | category | flops | bytes accessed | tf_op | source)
XLA Modules:
  0.0 39.4 jit_solution(7540180207779468528)
XLA Ops:
  0.6 36.2 %shard_map.127 = (f32[2,32,4096]{2,1,0:T(8,128)S(1)}, bf16[2,160,192]{2,1,0:T(8,128)(2,1)S(1)}, f32[2,128,4096]{2,1,0:T(8,128)S(1)}) custom-call(bf16[1,128,4096]{2,1,0:T(8,128)(2,1)} %g0.1, f32[1,32,128]{2,1,0:T(8,128)} %bitcast.8, bf16[1,128,4096]{2,1,0:T(8,128)(2,1)} %e0.1, f32[32,4096]{1,0:T(8,128)} %bitcast.6, bf16[1,128,4096]{2,1,0:T(8,128)(2,1)} %g1.1, ...), custom_call_target="tpu_custom_call" | custom-call | flops 1073741824 | bytes 8388608 | tf_op jit(solution)/shard_map/pallas_call | solution.py:339
  36.9 2.5 %shard_map.128 = (f32[32,4096]{1,0:T(8,128)}, f32[32,4096]{1,0:T(8,128)}, bf16[128,4096]{1,0:T(8,128)(2,1)}, bf16[128,4096]{1,0:T(8,128)(2,1)}, bf16[1,128,4096]...) custom-call(f32[2,32,4096]{2,1,0:T(8,128)S(1)} %get-tuple-element.15.sums, bf16[2,160,192]{2,1,0:T(8,128)(2,1)S(1)} %get-tuple-element.16.left, ...), custom_call_target="tpu_custom_call" | custom-call | tf_op jit(solution)/shard_map/pallas_call | solution.py:407

commit v6 on v5

--- a/solution.py
+++ b/solution.py
@@ -161,20 +161,21 @@
             total_wait(g_buf.at[m, :, cols], in_sems.at[m, k, 0])
             total_wait(e_buf.at[m, :, cols], in_sems.at[m, k, 1])
         result = []
-        zero = jnp.zeros((ROWS, BLOCK), BF16)
+        zero = jnp.zeros((2 * RANK, BLOCK), BF16)
+        lower = lax.broadcasted_iota(jnp.int32, (ROWS, 4 * RANK), 1) < 2 * RANK
         for m in range(2):
             total = totals[m]
             scale = s_buf[m, pl.ds(pl.multiple_of(k * count, count), count), :].T
             for b in range(0, count, 2):
                 at = pl.ds(pl.multiple_of(k * LOAD + b * BLOCK, 2 * BLOCK), 2 * BLOCK)
-                hi, mid, lo = split3(p_buf[m, :, at])
-                prior = jnp.concatenate([hi, mid, lo, jnp.zeros_like(hi)], 0)
+                hi, lo = split2(p_buf[m, :, at])
+                prior = jnp.concatenate([hi, lo], 0)
                 even = jnp.concatenate([prior[:, :BLOCK], zero], 1)
                 odd = jnp.concatenate([zero, prior[:, BLOCK:]], 1)
                 both = jnp.concatenate([g_buf[m, :, at], e_buf[m, :, at]], 0)
                 out = mm(both, jnp.concatenate([even, odd], 0), NT)
-                scaled = out[:ROWS, :128] * scale[:, b : b + 1] + out[:ROWS, 128:] * scale[:, b + 1 : b + 2]
-                total = total + (scaled + (out[ROWS:, :128] + out[ROWS:, 128:]))
+                pair = jnp.where(lower, scale[:, b : b + 1], scale[:, b + 1 : b + 2])
+                total = total + (out[:ROWS] * pair + out[ROWS:])
             result.append(total)
         return tuple(result)
 
@@ -182,7 +183,8 @@
     totals = lax.fori_loop(0, LOADS, partial, (start, start))
     for m in range(2):
         total = totals[m]
-        factor = total[:, :RANK] + (total[:, RANK : 2 * RANK] + total[:, 2 * RANK : 3 * RANK])
+        folded = total[:, : 2 * RANK] + total[:, 2 * RANK :]
+        factor = folded[:, :RANK] + folded[:, RANK:]
         f_part[m] = factor.T
 
     pl.semaphore_wait(barrier, NZ + (NXY - 1))

time: 39.6 us -> 39.6 us (level)
  no operation moved by 1% of the time
where the time goes in v6:
time: 39.6 us; the launch traced here: 39.4 us
  Pallas kernels  38.7 us (98%)
  between operations  0.64 us (2%)
    pallas_call x1, Pallas kernels, exchange(): pl.pallas_call(exchange_kernel, out_shape=(jax.ShapeDtypeStruct((2, RANK,...  36.2 us
    pallas_call x1, Pallas kernels, finish(): pl.pallas_call(finish_kernel, out_shape=(jax.ShapeDtypeStruct((RANK, COLS...  2.54 us

profile of v6, /device:TPU:1, one launch (start us, length us, event | category | flops | bytes accessed | tf_op | source)
XLA Modules:
  0.0 39.4 jit_solution(5144309457590819392)
XLA Ops:
  0.6 36.2 %shard_map.127 = (f32[2,32,4096]{2,1,0:T(8,128)S(1)}, bf16[2,160,192]{2,1,0:T(8,128)(2,1)S(1)}, f32[2,128,4096]{2,1,0:T(8,128)S(1)}) custom-call(bf16[1,128,4096]{2,1,0:T(8,128)(2,1)} %g0.1, f32[1,32,128]{2,1,0:T(8,128)} %bitcast.8, bf16[1,128,4096]{2,1,0:T(8,128)(2,1)} %e0.1, f32[32,4096]{1,0:T(8,128)} %bitcast.6, bf16[1,128,4096]{2,1,0:T(8,128)(2,1)} %g1.1, ...), custom_call_target="tpu_custom_call" | custom-call | flops 1073741824 | bytes 8388608 | tf_op jit(solution)/shard_map/pallas_call | solution.py:341
  36.8 2.5 %shard_map.128 = (f32[32,4096]{1,0:T(8,128)}, f32[32,4096]{1,0:T(8,128)}, bf16[128,4096]{1,0:T(8,128)(2,1)}, bf16[128,4096]{1,0:T(8,128)(2,1)}, bf16[1,128,4096]...) custom-call(f32[2,32,4096]{2,1,0:T(8,128)S(1)} %get-tuple-element.15.sums, bf16[2,160,192]{2,1,0:T(8,128)(2,1)S(1)} %get-tuple-element.16.left, ...), custom_call_target="tpu_custom_call" | custom-call | tf_op jit(solution)/shard_map/pallas_call | solution.py:409
